TPU v7x, 32 devices: a whole 2x2x4 slice. The times are simulated.
32 devices in a mesh: dp: 16 (over z, y, x), tensor: 2 (over core).
Axes of the slice: x: 2, y: 2, z: 4, core: 2. Of those that a mesh axis runs over, the one named last changes fastest.
Arguments:
- decoder_input: bfloat16 [16, 1024, 768], P('dp'), may hold values from -6 to 6
- encoder_output: bfloat16 [16, 512, 768], P('dp'), may hold values from -6 to 6
- cotangent: bfloat16 [16, 1024, 768], P('dp'), may hold values from -6 to 6
- target_length: int32 [16], P('dp'), may hold values from 128 to 1024, as said below
- source_length: int32 [16], P('dp'), may hold values from 128 to 512, as said below
- identifier_tags: int32 [16, 1024], P('dp'), may hold values 0 or 1
- distance_bucket: int32 [1024], replicated, may hold values from 0 to 31, as said below
- self_gain: float32 [768], replicated, may hold values from 0.5 to 1.5
- self_query: bfloat16 [768, 768], P(None, 'tensor'), may hold values from -0.0546875 to 0.0546875
- self_attention_key: bfloat16 [768, 768], P(None, 'tensor'), may hold values from -0.21875 to 0.21875
- self_value: bfloat16 [768, 768], P(None, 'tensor'), may hold values from -0.21875 to 0.21875
- self_output: bfloat16 [768, 768], P('tensor'), may hold values from -1.25 to 1.25
- position_table: float32 [32, 12], P(None, 'tensor'), may hold values from -4 to 4
- cross_gain: float32 [768], replicated, may hold values from 0.5 to 1.5
- cross_query: bfloat16 [768, 768], P(None, 'tensor'), may hold values from -0.0546875 to 0.0546875
- cross_key: bfloat16 [768, 768], P(None, 'tensor'), may hold values from -0.21875 to 0.21875
- cross_value: bfloat16 [768, 768], P(None, 'tensor'), may hold values from -0.21875 to 0.21875
- cross_output: bfloat16 [768, 768], P('tensor'), may hold values from -1.25 to 1.25
- hidden_gain: float32 [768], replicated, may hold values from 0.5 to 1.5
- hidden_in: bfloat16 [768, 3072], P(None, 'tensor'), may hold values from -0.21875 to 0.21875
- hidden_out: bfloat16 [3072, 768], P('tensor'), may hold values from -0.109375 to 0.109375
Outputs:
- layer_out: bfloat16 [16, 1024, 768], P('dp')
- grad_decoder: float32 [16, 1024, 768], P('dp')
- grad_encoder: float32 [16, 512, 768], P('dp')
- grad_self_gain: float32 [768], replicated
- grad_self_query: float32 [768, 768], P(None, 'tensor')
- grad_self_key: float32 [768, 768], P(None, 'tensor')
- grad_self_value: float32 [768, 768], P(None, 'tensor')
- grad_self_output: float32 [768, 768], P('tensor')
- grad_position_table: float32 [32, 12], P(None, 'tensor')
- grad_cross_gain: float32 [768], replicated
- grad_cross_query: float32 [768, 768], P(None, 'tensor')
- grad_cross_key: float32 [768, 768], P(None, 'tensor')
- grad_cross_value: float32 [768, 768], P(None, 'tensor')
- grad_cross_output: float32 [768, 768], P('tensor')
- grad_hidden_gain: float32 [768], replicated
- grad_hidden_in: float32 [768, 3072], P(None, 'tensor')
- grad_hidden_out: float32 [3072, 768], P('tensor')
Inputs may be any that keep to these rules, and one draw needn't show every extreme that they name: `target_length`: some item has 1024 target tokens in every draw. `source_length`: some item has 512 encoder tokens in every draw. `distance_bucket`: Non-decreasing in the distance; equal to the distance below 16; 31 at distance 1024 - 1.
All inputs are finite; a program needn't handle non-finite values. No bound on the sum of `identifier_tags` on one device may be relied on, other than what follows from the above.
Results may differ from a plain program's by a relative error of at most 0.024.
The roundings to bfloat16 on the way count: a program that leaves them out, or rounds other values in their place, can miss the bound.
Values sent between devices are 32-bit elements; how exact they have to be, the bound alone decides.
No kernel may reach another device: no remote copies, remote signals or barrier semaphores. Data moves between devices by JAX's collectives and lax.ppermute only.
A program may use at most 256 MiB of HBM per device.

v0:
```python
from functools import partial

import jax
import jax.numpy as jnp
from jax import lax
from jax.sharding import PartitionSpec as P

EPSILON = 1e-06
MASKED = -1e30
FULL_ACCURACY = lax.Precision.HIGHEST


def matrix_product(former, latter):
    return jnp.dot(former, latter, preferred_element_type=jnp.float32)


def left_contract(former, latter):
    return jnp.einsum("ti,tj->ij", former, latter, preferred_element_type=jnp.float32)


def right_contract(former, latter):
    return jnp.einsum("ti,ji->tj", former, latter, preferred_element_type=jnp.float32)


def normalize(hidden, norm_gain):
    inverse_rms = lax.rsqrt(jnp.mean(hidden * hidden, axis=-1, keepdims=True) + EPSILON)
    return (hidden * inverse_rms * norm_gain, inverse_rms)


def norm_back(hidden, inverse_rms, norm_gain, grad_normed):
    grad_gain = jnp.sum(grad_normed * hidden * inverse_rms, axis=0)
    grad_scaled = grad_normed * norm_gain
    inner_sum = jnp.mean(grad_scaled * hidden, axis=-1, keepdims=True)
    cubed = inverse_rms * inverse_rms * inverse_rms
    return (inverse_rms * grad_scaled - hidden * cubed * inner_sum, grad_gain)


def bucket_table(distance_bucket, block_start, row_count, key_total, bucket_total):
    bucket_ids = jnp.arange(bucket_total + 1, dtype=jnp.int32)
    starts = jnp.sum((distance_bucket[None, :] < bucket_ids[:, None]).astype(jnp.int32), axis=1)
    rows_at = block_start + jnp.arange(row_count, dtype=jnp.int32)[:, None]
    cols_at = jnp.arange(key_total, dtype=jnp.int32)[None, :]
    distance = jnp.clip(rows_at - cols_at, 0, key_total - 1)
    return (distance[None] >= starts[:bucket_total, None, None]) & (
        distance[None] < starts[1:, None, None]
    )


def lookup_bias(position_bias_grid, one_hot_encoding):
    return jnp.einsum(
        "ptn,po->otn",
        one_hot_encoding.astype(jnp.float32),
        position_bias_grid,
        precision=FULL_ACCURACY,
    )


def causal_mask(length_limit, key_total):

    def allowed(block_start, row_count):
        rows_at = block_start + jnp.arange(row_count, dtype=jnp.int32)[:, None]
        cols_at = jnp.arange(key_total, dtype=jnp.int32)[None, :]
        return (cols_at <= rows_at) & (cols_at < length_limit)

    return allowed


def source_mask(length_limit, key_total):

    def allowed(block_start, row_count):
        cols_at = jnp.arange(key_total, dtype=jnp.int32)[None, :]
        return jnp.broadcast_to(cols_at < length_limit, (row_count, key_total))

    return allowed


def split_heads(matrix, head_count):
    return matrix.reshape(matrix.shape[0], head_count, matrix.shape[1] // head_count)


def block_scores(query_block, key_rows, head_count, bias_term, allowed):
    scores = jnp.einsum(
        "qhd,khd->hqk",
        split_heads(query_block, head_count),
        split_heads(key_rows, head_count),
        preferred_element_type=jnp.float32,
    )
    return jnp.where(allowed[None], scores + bias_term, MASKED)


def forward_layer_pass(query_block, key_rows, value_rows, head_count, bias_term, allowed):
    scores = block_scores(query_block, key_rows, head_count, bias_term, allowed)
    row_top = jnp.max(scores, axis=-1, keepdims=True)
    raised = jnp.exp(scores - row_top)
    row_total = jnp.sum(raised, axis=-1, keepdims=True)
    shares = (raised / row_total).astype(jnp.bfloat16)
    mixed = jnp.einsum(
        "hqk,khd->qhd",
        shares,
        split_heads(value_rows, head_count),
        preferred_element_type=jnp.float32,
    )
    return (
        mixed.reshape(query_block.shape[0], -1).astype(jnp.bfloat16),
        (row_top + jnp.log(row_total))[..., 0],
    )


def backward_block(
    query_block, key_rows, value_rows, grad_block, log_total, head_count, bias_term, allowed
):
    scores = block_scores(query_block, key_rows, head_count, bias_term, allowed)
    shares = jnp.exp(scores - log_total[..., None])
    grad_heads = split_heads(grad_block, head_count)
    grad_shares = jnp.einsum(
        "qhd,khd->hqk",
        grad_heads,
        split_heads(value_rows, head_count),
        preferred_element_type=jnp.float32,
    )
    grad_values = jnp.einsum(
        "hqk,qhd->khd", shares.astype(jnp.bfloat16), grad_heads, preferred_element_type=jnp.float32
    )
    inner_sum = jnp.sum(shares * grad_shares, axis=-1, keepdims=True)
    grad_scores = (shares * (grad_shares - inner_sum)).astype(jnp.bfloat16)
    grad_queries = jnp.einsum(
        "hqk,khd->qhd",
        grad_scores,
        split_heads(key_rows, head_count),
        preferred_element_type=jnp.float32,
    )
    grad_keys = jnp.einsum(
        "hqk,qhd->khd",
        grad_scores,
        split_heads(query_block, head_count),
        preferred_element_type=jnp.float32,
    )
    row_count = query_block.shape[0]
    key_total = key_rows.shape[0]
    return (
        grad_queries.reshape(row_count, -1),
        grad_keys.reshape(key_total, -1),
        grad_values.reshape(key_total, -1),
        grad_scores,
    )


def attend_item(
    queries, key_rows, value_rows, head_count, allowed, position_bias_grid, distance_bucket
):
    row_count = queries.shape[0]
    block_size = min(512, row_count)
    outputs = []
    log_totals = []
    for block_start in range(0, row_count, block_size):
        if position_bias_grid is None:
            bias_term = 0.0
        else:
            one_hot_encoding = bucket_table(
                distance_bucket,
                block_start,
                block_size,
                key_rows.shape[0],
                position_bias_grid.shape[0],
            )
            bias_term = lookup_bias(position_bias_grid, one_hot_encoding)
        mixed, log_total = forward_layer_pass(
            queries[block_start : block_start + block_size],
            key_rows,
            value_rows,
            head_count,
            bias_term,
            allowed(block_start, block_size),
        )
        outputs.append(mixed)
        log_totals.append(log_total)
    return (jnp.concatenate(outputs, axis=0), log_totals)


def attend_back(
    queries,
    key_rows,
    value_rows,
    grad_mixed,
    log_totals,
    head_count,
    allowed,
    position_bias_grid,
    distance_bucket,
):
    row_count = queries.shape[0]
    key_total = key_rows.shape[0]
    block_size = min(512, row_count)
    query_parts = []
    grad_key_rows = jnp.zeros(key_rows.shape, jnp.float32)
    grad_value_rows = jnp.zeros(value_rows.shape, jnp.float32)
    grad_table = (
        None if position_bias_grid is None else jnp.zeros(position_bias_grid.shape, jnp.float32)
    )
    for block_number, block_start in enumerate(range(0, row_count, block_size)):
        if position_bias_grid is None:
            bias_term = 0.0
        else:
            one_hot_encoding = bucket_table(
                distance_bucket, block_start, block_size, key_total, position_bias_grid.shape[0]
            )
            bias_term = lookup_bias(position_bias_grid, one_hot_encoding)
        grad_queries, grad_keys, grad_values, grad_scores = backward_block(
            queries[block_start : block_start + block_size],
            key_rows,
            value_rows,
            grad_mixed[block_start : block_start + block_size],
            log_totals[block_number],
            head_count,
            bias_term,
            allowed(block_start, block_size),
        )
        query_parts.append(grad_queries)
        grad_key_rows = grad_key_rows + grad_keys
        grad_value_rows = grad_value_rows + grad_values
        if position_bias_grid is not None:
            grad_table = grad_table + jnp.einsum(
                "dju,cju->cd",
                grad_scores,
                one_hot_encoding.astype(jnp.bfloat16),
                preferred_element_type=jnp.float32,
            )
    return (jnp.concatenate(query_parts, axis=0), grad_key_rows, grad_value_rows, grad_table)


def body(
    decoder_input,
    encoder_output,
    cotangent,
    target_length,
    source_length,
    identifier_tags,
    distance_bucket,
    self_gain,
    self_query,
    self_attention_key,
    self_value,
    self_output,
    position_table,
    cross_gain,
    cross_query,
    cross_key,
    cross_value,
    cross_output,
    hidden_gain,
    hidden_in,
    hidden_out,
):
    item_count, target, model_width = decoder_input.shape
    source = encoder_output.shape[1]
    head_count = position_table.shape[1]
    decoder_rows = decoder_input.reshape(item_count * target, model_width).astype(jnp.float32)
    encoder_rows = encoder_output.reshape(item_count * source, model_width)
    normed_one, rms_one = normalize(decoder_rows, self_gain)
    input_one = normed_one.astype(jnp.bfloat16)
    queries_one = matrix_product(input_one, self_query).astype(jnp.bfloat16)
    keys_one = matrix_product(input_one, self_attention_key).astype(jnp.bfloat16)
    first_value_rows = matrix_product(input_one, self_value).astype(jnp.bfloat16)
    mixed_parts = []
    number = 0
    mixed, log_totals = attend_item(
        queries_one,
        keys_one,
        first_value_rows,
        head_count,
        causal_mask(target_length[number], target),
        position_table,
        distance_bucket,
    )
    mixed_parts.append(mixed)
    totals_one = [log_totals]
    mixed_one = mixed_parts[0]
    self_branch = lax.psum(matrix_product(mixed_one, self_output), "tensor")
    first = decoder_rows + self_branch
    second_normalized, rms_two = normalize(first, cross_gain)
    input_two = second_normalized.astype(jnp.bfloat16)
    queries_two = matrix_product(input_two, cross_query).astype(jnp.bfloat16)
    keys_two = matrix_product(encoder_rows, cross_key).astype(jnp.bfloat16)
    values_two = matrix_product(encoder_rows, cross_value).astype(jnp.bfloat16)
    mixed_parts = []
    number = 0
    mixed, log_totals = attend_item(
        queries_two,
        keys_two,
        values_two,
        head_count,
        source_mask(source_length[number], source),
        None,
        distance_bucket,
    )
    mixed_parts.append(mixed)
    totals_two = [log_totals]
    mixed_two = mixed_parts[0]
    cross_branch = lax.psum(matrix_product(mixed_two, cross_output), "tensor")
    second = first + cross_branch
    normed_three, rms_three = normalize(second, hidden_gain)
    input_three = normed_three.astype(jnp.bfloat16)
    before = matrix_product(input_three, hidden_in)
    gelu_tanh = partial(jax.nn.gelu, approximate=True)
    active = gelu_tanh(before).astype(jnp.bfloat16)
    hidden_branch = lax.psum(matrix_product(active, hidden_out), "tensor")
    third = second + hidden_branch
    layer_out = third.astype(jnp.bfloat16).reshape(item_count, target, model_width)
    places = jnp.arange(target, dtype=jnp.int32)
    factor = jnp.where(
        places[None, :] < target_length[:, None], 1.0 + identifier_tags.astype(jnp.float32), 0.0
    )
    grad_third = (cotangent.astype(jnp.float32) * factor[:, :, None]).reshape(
        item_count * target, model_width
    )
    grad_branch = grad_third.astype(jnp.bfloat16)
    grad_hidden_out = left_contract(active, grad_branch)
    grad_active = right_contract(grad_branch, hidden_out)
    gelu_value, gelu_pull = jax.vjp(gelu_tanh, before)
    grad_before = gelu_pull(grad_active)[0].astype(jnp.bfloat16)
    grad_hidden_in = left_contract(input_three, grad_before)
    grad_input_three = lax.psum(right_contract(grad_before, hidden_in), "tensor")
    back_three, grad_hidden_gain = norm_back(second, rms_three, hidden_gain, grad_input_three)
    grad_second = grad_third + back_three
    grad_branch_two = grad_second.astype(jnp.bfloat16)
    grad_cross_output = left_contract(mixed_two, grad_branch_two)
    grad_mixed_two = right_contract(grad_branch_two, cross_output).astype(jnp.bfloat16)
    query_parts = []
    key_parts = []
    value_parts = []
    number = 0
    grad_queries, grad_keys, grad_values, unused_table = attend_back(
        queries_two,
        keys_two,
        values_two,
        grad_mixed_two,
        totals_two[number],
        head_count,
        source_mask(source_length[number], source),
        None,
        distance_bucket,
    )
    query_parts.append(grad_queries)
    key_parts.append(grad_keys)
    value_parts.append(grad_values)
    grad_queries_two = query_parts[0].astype(jnp.bfloat16)
    grad_keys_two = key_parts[0].astype(jnp.bfloat16)
    grad_values_two = value_parts[0].astype(jnp.bfloat16)
    grad_cross_query = left_contract(input_two, grad_queries_two)
    grad_cross_key = left_contract(encoder_rows, grad_keys_two)
    grad_cross_value = left_contract(encoder_rows, grad_values_two)
    grad_input_two, grad_encoder = lax.psum(
        (
            right_contract(grad_queries_two, cross_query),
            right_contract(grad_keys_two, cross_key) + right_contract(grad_values_two, cross_value),
        ),
        "tensor",
    )
    back_two, grad_cross_gain = norm_back(first, rms_two, cross_gain, grad_input_two)
    grad_first = grad_second + back_two
    grad_branch_one = grad_first.astype(jnp.bfloat16)
    grad_self_output = left_contract(mixed_one, grad_branch_one)
    grad_mixed_one = right_contract(grad_branch_one, self_output).astype(jnp.bfloat16)
    query_parts = []
    key_parts = []
    value_parts = []
    number = 0
    grad_queries, grad_keys, grad_values, grad_table = attend_back(
        queries_one,
        keys_one,
        first_value_rows,
        grad_mixed_one,
        totals_one[number],
        head_count,
        causal_mask(target_length[number], target),
        position_table,
        distance_bucket,
    )
    query_parts.append(grad_queries)
    key_parts.append(grad_keys)
    value_parts.append(grad_values)
    grad_queries_one = query_parts[0].astype(jnp.bfloat16)
    grad_keys_one = key_parts[0].astype(jnp.bfloat16)
    grad_values_one = value_parts[0].astype(jnp.bfloat16)
    grad_self_query = left_contract(input_one, grad_queries_one)
    grad_self_key = left_contract(input_one, grad_keys_one)
    grad_self_value = left_contract(input_one, grad_values_one)
    grad_input_one = lax.psum(
        right_contract(grad_queries_one, self_query)
        + right_contract(grad_keys_one, self_attention_key)
        + right_contract(grad_values_one, self_value),
        "tensor",
    )
    back_one, grad_self_gain = norm_back(decoder_rows, rms_one, self_gain, grad_input_one)
    grad_decoder = (grad_first + back_one).reshape(item_count, target, model_width)
    grad_encoder = grad_encoder.reshape(item_count, source, model_width)
    every_sum = lax.psum(
        (
            grad_self_gain,
            grad_self_query,
            grad_self_key,
            grad_self_value,
            grad_self_output,
            grad_table,
            grad_cross_gain,
            grad_cross_query,
            grad_cross_key,
            grad_cross_value,
            grad_cross_output,
            grad_hidden_gain,
            grad_hidden_in,
            grad_hidden_out,
        ),
        "dp",
    )
    return (
        layer_out,
        grad_decoder,
        grad_encoder,
        every_sum[0],
        every_sum[1],
        every_sum[2],
        every_sum[3],
        every_sum[4],
        every_sum[5],
        every_sum[6],
        every_sum[7],
        every_sum[8],
        every_sum[9],
        every_sum[10],
        every_sum[11],
        every_sum[12],
        every_sum[13],
    )


def solution(mesh):
    placed = (
        P("dp", None, None),
        P("dp", None, None),
        P("dp", None, None),
        P("dp"),
        P("dp"),
        P("dp", None),
        P(),
        P(),
        P(None, "tensor"),
        P(None, "tensor"),
        P(None, "tensor"),
        P("tensor", None),
        P(None, "tensor"),
        P(),
        P(None, "tensor"),
        P(None, "tensor"),
        P(None, "tensor"),
        P("tensor", None),
        P(),
        P(None, "tensor"),
        P("tensor", None),
    )
    return jax.shard_map(
        body,
        mesh=mesh,
        in_specs=placed,
        out_specs=(
            P("dp", None, None),
            P("dp", None, None),
            P("dp", None, None),
            P(),
            P(None, "tensor"),
            P(None, "tensor"),
            P(None, "tensor"),
            P("tensor", None),
            P(None, "tensor"),
            P(),
            P(None, "tensor"),
            P(None, "tensor"),
            P(None, "tensor"),
            P("tensor", None),
            P(),
            P(None, "tensor"),
            P("tensor", None),
        ),
        check_vma=False,
    )
```

profile of v0, /device:TPU:0, one launch (start us, length us, event | category | flops | bytes accessed | tf_op | source)
XLA Modules:
  0.0 944.3 jit_solution(4503293925115913269)
XLA Ops:
  15.5 25.6 %fusion.1 = f32[512,1024,6]{1,2,0:T(8,128)} fusion(s32[512,1024]{1,0:T(8,128)S(1)} %subtract_clamp_fusion.1, s32[32]{0:T(128)S(1)} %get-tuple-element.101, s32[32]{0:T(128)S(1)} %get-tuple-element.100, f32[32,6]{0,1:T(8,128)S(1)} %copy-done.133), kind=kOutput, calls=%fused_computation.3 | convolution fusion | flops 1258291200 | bytes 14681088 | tf_op jit(solution)/shard_map/ptn,po->otn/dot_general | solution.py:50
  41.0 25.7 %fusion.3 = f32[512,1024,6]{1,2,0:T(8,128)} fusion(s32[512,1024]{1,0:T(8,128)S(1)} %subtract_clamp_fusion, s32[32]{0:T(128)S(1)} %get-tuple-element.101, s32[32]{0:T(128)S(1)} %get-tuple-element.100, f32[32,6]{0,1:T(8,128)S(1)} %copy-done.133), kind=kOutput, calls=%fused_computation.5 | convolution fusion | flops 1258291200 | bytes 14681088 | tf_op jit(solution)/shard_map/ptn,po->otn/dot_general | solution.py:50
  66.8 14.5 %fusion.149 = (f32[6,512]{1,0:T(8,128)S(1)}, f32[6,512,1024]{2,1,0:T(8,128)S(1)}) fusion(f32[512,1024,6]{1,2,0:T(8,128)} %fusion.1, bf16[512,6,64]{0,2,1:T(8,128)(2,1)S(1)} %bitcast.240, bf16[1024,6,64]{0,2,1:T(8,128)(2,1)S(1)} %bitcast.226, pred[512,1024]{1,0:T(8,128)(4,1)S(1)} %get-tuple-element.96), kind=kOutput, calls=%fused_computation.216 | convolution fusion | flops 412087296 | bytes 26882048 | tf_op jit(solution)/shard_map/qhd,khd->hqk/dot_general | solution.py:82
  81.3 3.0 fusion.18
  85.9 3.3 fusion.89
  89.3 14.7 %fusion.148 = (f32[6,512]{1,0:T(8,128)S(1)}, f32[6,512,1024]{2,1,0:T(8,128)S(1)}) fusion(f32[512,1024,6]{1,2,0:T(8,128)} %fusion.3, bf16[512,6,64]{0,2,1:T(8,128)(2,1)S(1)} %bitcast.238, bf16[1024,6,64]{0,2,1:T(8,128)(2,1)S(1)} %bitcast.227, pred[512,1024]{1,0:T(8,128)(4,1)S(1)} %get-tuple-element.97), kind=kOutput, calls=%fused_computation.215 | convolution fusion | flops 412087296 | bytes 26882048 | tf_op jit(solution)/shard_map/qhd,khd->hqk/dot_general | solution.py:82
  103.9 2.8 fusion.19
  108.7 3.3 fusion.88
  112.8 2.7 fusion.116
  120.5 21.0 %all-reduce.10.cloned.1.call-done = f32[1024,768]{1,0:T(8,128)} async-done(((f32[1024,768]{1,0:T(8,128)}), f32[1024,768]{1,0:T(8,128)}) %all-reduce.10.cloned.1.call-update) | async-done | bytes 3145744 | tf_op jit(solution)/shard_map/psum | solution.py:278
  141.5 2.8 multiply_reduce_fusion.9
  147.4 2.6 fusion.39
  155.2 2.7 fusion.115
  158.6 23.8 %all-reduce.12.cloned.1.call-done = f32[1024,768]{1,0:T(8,128)} async-done(((f32[1024,768]{1,0:T(8,128)}), f32[1024,768]{1,0:T(8,128)}) %all-reduce.12.cloned.1.call-update) | async-done | bytes 3145744 | tf_op jit(solution)/shard_map/psum | solution.py:299
  182.4 3.3 multiply_reduce_fusion.8
  187.4 2.7 fusion.136
  190.1 6.1 fusion.30
  197.9 4.3 fusion.150
  205.1 21.6 %all-reduce.14.cloned.1.call-done = f32[1024,768]{1,0:T(8,128)} async-done(((f32[1024,768]{1,0:T(8,128)}), f32[1024,768]{1,0:T(8,128)}) %all-reduce.14.cloned.1.call-update) | async-done | bytes 3145744 | tf_op jit(solution)/shard_map/psum | solution.py:322
  226.7 3.4 multiply_reduce_fusion.4
  236.6 5.2 multiply_reduce_fusion.3
  241.8 7.7 multiply_convert_fusion.3
  249.5 2.7 convolution_convert_fusion.9
  253.7 2.6 fusion.114
  257.5 9.0 fusion.137
  275.3 5.7 all-reduce.16.cloned.1.call-done
  281.0 3.4 multiply_reduce_fusion.5
  284.4 3.6 subtract_add_fusion
  291.5 6.3 multiply_reduce_fusion.1
  297.8 10.0 %multiply_convert_fusion.1 = bf16[6,512,1024]{2,1,0:T(8,128)(2,1)} fusion(f32[6,512,1024]{2,1,0:T(8,128)} %get-tuple-element.113, f32[6,512,1024]{2,1,0:T(8,128)S(1)} %bitcast.213, f32[6,512]{1,0:T(8,128)S(1)} %get-tuple-element.112, f32[6,512]{1,0:T(8,128)S(1)} %copy-done.98), kind=kLoop, calls=%fused_computation.25 | loop fusion | flops 12582912 | bytes 31481856 | tf_op jit(solution)/shard_map/convert_element_type | solution.py:125
  307.9 5.8 convolution_convert_fusion.7
  313.7 5.2 fusion.152
  318.9 3.2 fusion.31
  322.2 7.5 multiply_reduce_fusion
  329.7 4.6 add_convert_fusion.1
  334.3 6.3 multiply_convert_fusion
  347.3 2.7 add_add_fusion
  350.5 8.5 fusion.135
  359.1 10.4 %fusion.109 = f32[1536,768]{1,0:T(8,128)} fusion(bf16[1,1024,768]{2,1,0:T(8,128)(2,1)S(1)} %copy-done.71, f32[1024]{0:T(1024)S(1)} %bitcast.288, f32[1024,1536]{1,0:T(8,128)} %copy-done.134), kind=kOutput, calls=%fused_computation.164 | convolution fusion | flops 2432434176 | bytes 12587008 | tf_op jit(solution)/shard_map/ti,tj->ij/dot_general | solution.py:18
  381.4 2.5 fusion.119
  387.1 18.3 %fusion.90 = f32[32,6]{0,1:T(8,128)S(1)} fusion(bf16[6,512,1024]{2,1,0:T(8,128)(2,1)} %copy-done.11, s32[512,1024]{1,0:T(8,128)} %copy-done.62, s32[32]{0:T(128)S(1)} %copy-done.131, s32[32]{0:T(128)S(1)} %copy-done.129), kind=kOutput, calls=%fused_computation.147 | convolution fusion | flops 251658240 | bytes 8389632 | tf_op jit(solution)/shard_map/dju,cju->cd/dot_general | solution.py:222
  405.5 19.8 %fusion.96 = f32[32,6]{0,1:T(8,128)S(1)} fusion(f32[32,6]{0,1:T(8,128)S(1)} %fusion.90, bf16[6,512,1024]{2,1,0:T(8,128)(2,1)S(1)} %bitcast.225, s32[512,1024]{1,0:T(8,128)S(1)} %copy-done.64, s32[32]{0:T(128)S(1)} %copy-done.131, s32[32]{0:T(128)S(1)} %copy-done.129), kind=kOutput, calls=%fused_computation.149 | convolution fusion | flops 251658432 | bytes 8390400 | tf_op jit(solution)/shard_map/dju,cju->cd/dot_general | solution.py:222
  425.3 3.8 fusion.58
  429.1 81.4 %all-reduce = (f32[768]{0:T(1024)}, f32[32,6]{0,1:T(8,128)}, f32[768]{0:T(1024)}, f32[768]{0:T(1024)}) all-reduce(f32[768]{0:T(1024)S(1)} %get-tuple-element.55, f32[32,6]{0,1:T(8,128)S(1)} %fusion.96, f32[768]{0:T(1024)S(1)} %copy-done.126, f32[768]{0:T(1024)S(1)} %copy-done.125), channel_id=1, replica_groups=mesh['dp'=16,'tensor'=2] {'dp'}, use_global_device_ids=true, to_apply=%region_27.28 | all-reduce | flops 2496 | bytes 19968 | tf_op jit(solution)/shard_map/psum | solution.py:397
  510.5 3.5 fusion.75
  517.5 400.4 %all-reduce.18.cloned.1.call-done = (f32[768,384]{1,0:T(8,128)}, f32[768,384]{1,0:T(8,128)}, f32[768,384]{1,0:T(8,128)}, f32[384,768]{1,0:T(8,128)}, f32[768,384...) async-done(((f32[768,384]{1,0:T(8,128)}, f32[768,384]{1,0:T(8,128)}, ...) | async-done | bytes 18874384 | tf_op jit(solution)/shard_map/psum | solution.py:397
  918.0 2.7 copy.64
  920.7 2.7 copy.65
  (397 shorter events, 90.7 us)
Async XLA Ops:
  7.2 180.2 %copy-start = (bf16[768,1536]{1,0:T(8,128)(2,1)S(1)}, bf16[768,1536]{1,0:T(8,128)(2,1)}, u32[]{:S(2)}) copy-start(bf16[768,1536]{1,0:T(8,128)(2,1)} %param.40) | copy-start | bytes 7077892
  7.2 134.3 %all-reduce.10.cloned.1.call-start = ((), (), s32[]{:S(2)}) async-start(), calls=%async_computation | async-start | bytes 6291456 | tf_op jit(solution)/shard_map/psum | solution.py:278
  7.6 7.9 copy-start.63
  10.2 30.8 %copy-start.128 = (s32[32]{0:T(128)}, s32[32]{0:T(128)S(1)}, u32[]{:S(2)}) copy-start(s32[32]{0:T(128)S(1)} %get-tuple-element.100) | copy-start | bytes 388
  10.2 30.8 %copy-start.130 = (s32[32]{0:T(128)}, s32[32]{0:T(128)S(1)}, u32[]{:S(2)}) copy-start(s32[32]{0:T(128)S(1)} %get-tuple-element.101) | copy-start | bytes 388
  12.3 54.5 %copy-start.31 = (bf16[512,384]{0,1:T(8,128)(2,1)}, bf16[512,384]{0,1:T(8,128)(2,1)S(1)}, u32[]{:S(2)}) copy-start(bf16[512,384]{0,1:T(8,128)(2,1)S(1)} %get-tuple-element.88) | copy-start | bytes 1179652
  12.3 76.9 %copy-start.29 = (bf16[512,384]{0,1:T(8,128)(2,1)}, bf16[512,384]{0,1:T(8,128)(2,1)S(1)}, u32[]{:S(2)}) copy-start(bf16[512,384]{0,1:T(8,128)(2,1)S(1)} %get-tuple-element.89) | copy-start | bytes 1179652
  13.5 75.8 %copy-start.25 = (bf16[1024,384]{0,1:T(8,128)(2,1)}, bf16[1024,384]{0,1:T(8,128)(2,1)S(1)}, u32[]{:S(2)}) copy-start(bf16[1024,384]{0,1:T(8,128)(2,1)S(1)} %convolution_convert_fusion.3) | copy-start | bytes 2359300
  14.5 92.3 %copy-start.49 = (bf16[1024,384]{0,1:T(8,128)(2,1)}, bf16[1024,384]{0,1:T(8,128)(2,1)S(1)}, u32[]{:S(2)}) copy-start(bf16[1024,384]{0,1:T(8,128)(2,1)S(1)} %convolution_convert_fusion.5) | copy-start | bytes 2359300
  14.9 26.1 %copy-start.62 = (s32[512,1024]{1,0:T(8,128)}, s32[512,1024]{1,0:T(8,128)S(1)}, u32[]{:S(2)}) copy-start(s32[512,1024]{1,0:T(8,128)S(1)} %subtract_clamp_fusion) | copy-start | bytes 6291460
  89.2 22.8 %copy-start.73 = (bf16[6,64,512]{2,1,0:T(8,128)(2,1)}, bf16[6,64,512]{2,1,0:T(8,128)(2,1)S(1)}, u32[]{:S(2)}) copy-start(bf16[6,64,512]{2,1,0:T(8,128)(2,1)S(1)} %fusion.89) | copy-start | bytes 1179652
  115.5 67.0 %all-reduce.12.cloned.1.call-start = ((), (), s32[]{:S(2)}) async-start(), calls=%async_computation.1 | async-start | bytes 6291456 | tf_op jit(solution)/shard_map/psum | solution.py:299
  116.6 36.2 %copy-start.115 = (pred[512]{0:T(512)(128)(4,1)}, pred[512]{0:T(512)(128)(4,1)S(1)}, u32[]{:S(2)}) copy-start(pred[512]{0:T(512)(128)(4,1)S(1)} %iota_compare_fusion.4) | copy-start | bytes 1540
  120.5 24.5 %copy-start.56 = (bf16[768,384]{1,0:T(8,128)(2,1)S(1)}, bf16[768,384]{1,0:T(8,128)(2,1)}, u32[]{:S(2)}) copy-start(bf16[768,384]{1,0:T(8,128)(2,1)} %param.35) | copy-start | bytes 1769476
  120.5 24.5 %copy-start.112 = (f32[768]{0:T(1024)S(1)}, f32[768]{0:T(1024)}, u32[]{:S(2)}) copy-start(f32[768]{0:T(1024)} %param.34) | copy-start | bytes 9220
  157.9 68.8 %all-reduce.14.cloned.1.call-start = ((), (), s32[]{:S(2)}) async-start(), calls=%async_computation.2 | async-start | bytes 6291456 | tf_op jit(solution)/shard_map/psum | solution.py:322
  158.6 31.5 %copy-start.118 = (f32[1,1024]{1,0:T(1,128)}, f32[1,1024]{1,0:T(1,128)S(1)}, u32[]{:S(2)}) copy-start(f32[1,1024]{1,0:T(1,128)S(1)} %compare_select_fusion) | copy-start | bytes 12292
  158.6 28.8 %copy-start.97 = (f32[768]{0:T(1024)S(1)}, f32[768]{0:T(1024)}, u32[]{:S(2)}) copy-start(f32[768]{0:T(1024)} %param.39) | copy-start | bytes 9220
  202.2 24.6 %copy-start.9 = (f32[1024,768]{1,0:T(8,128)S(1)}, f32[1024,768]{1,0:T(8,128)}, u32[]{:S(2)}) copy-start(f32[1024,768]{1,0:T(8,128)} %copy-done.8) | copy-start | bytes 9437188
  202.2 78.8 %all-reduce.16.cloned.1.call-start = ((), (), s32[]{:S(2)}) async-start(), calls=%async_computation.3 | async-start | bytes 6291456 | tf_op jit(solution)/shard_map/psum | solution.py:352
  256.4 13.4 %slice-start.12 = ((s8[6291456]{0:T(1024)(128)(4,1)}), s8[2097152]{0:T(1024)(128)(4,1)S(1)}, s32[]{:S(2)}) async-start(s8[6291456]{0:T(1024)(128)(4,1)} %bitcast.222), calls=%async_computation.18 | async-start | bytes 4194304
  256.4 168.9 %all-reduce.20.cloned.1.call-start = ((), (), s32[]{:S(2)}) async-start(), calls=%async_computation.5 | async-start | bytes 15728640 | tf_op jit(solution)/shard_map/psum | solution.py:306
  257.5 9.0 copy-start.19
  257.5 9.0 copy-start.36
  257.5 10.1 %copy-start.18 = (bf16[6,512,512]{1,2,0:T(8,128)(2,1)S(1)}, bf16[6,512,512]{1,2,0:T(8,128)(2,1)}, u32[]{:S(2)}) copy-start(bf16[6,512,512]{1,2,0:T(8,128)(2,1)} %get-tuple-element.99) | copy-start | bytes 9437188
  257.5 10.1 %copy-start.44 = (bf16[512,384]{0,1:T(8,128)(2,1)S(1)}, bf16[512,384]{0,1:T(8,128)(2,1)}, u32[]{:S(2)}) copy-start(bf16[512,384]{0,1:T(8,128)(2,1)} %copy-done.43) | copy-start | bytes 1179652
  257.5 12.3 %slice-start.13 = ((s8[6291456]{0:T(1024)(128)(4,1)}), s8[4194304]{0:T(1024)(128)(4,1)S(1)}, s32[]{:S(2)}) async-start(s8[6291456]{0:T(1024)(128)(4,1)} %bitcast.222), calls=%async_computation.19 | async-start | bytes 8388608
  272.8 8.2 copy-start.7
  281.0 8.7 slice-start
  284.4 6.9 slice-start.2
  288.0 9.8 %copy-start.12 = (f32[1024,768]{1,0:T(8,128)}, f32[1024,768]{1,0:T(8,128)S(1)}, u32[]{:S(2)}) copy-start(f32[1024,768]{1,0:T(8,128)S(1)} %subtract_add_fusion) | copy-start | bytes 9437188
  289.7 8.1 copy-start.47
  297.8 10.1 %copy-start.26 = (bf16[1024,384]{0,1:T(8,128)(2,1)S(1)}, bf16[1024,384]{0,1:T(8,128)(2,1)}, u32[]{:S(2)}) copy-start(bf16[1024,384]{0,1:T(8,128)(2,1)} %copy-done.25) | copy-start | bytes 2359300
  297.8 21.1 %slice-start.3 = ((s8[12582912]{0:T(1024)(128)(4,1)}), s8[4194304]{0:T(1024)(128)(4,1)S(1)}, s32[]{:S(2)}) async-start(s8[12582912]{0:T(1024)(128)(4,1)} %bitcast.214), calls=%async_computation.9 | async-start | bytes 8388608
  297.8 21.1 %slice-start.4 = ((s8[12582912]{0:T(1024)(128)(4,1)}), s8[4194304]{0:T(1024)(128)(4,1)S(1)}, s32[]{:S(2)}) async-start(s8[12582912]{0:T(1024)(128)(4,1)} %bitcast.214), calls=%async_computation.10 | async-start | bytes 8388608
  307.9 11.0 %slice-start.5 = ((s8[12582912]{0:T(1024)(128)(4,1)}), s8[4194304]{0:T(1024)(128)(4,1)S(1)}, s32[]{:S(2)}) async-start(s8[12582912]{0:T(1024)(128)(4,1)} %bitcast.214), calls=%async_computation.11 | async-start | bytes 8388608
  350.1 567.9 %all-reduce.18.cloned.1.call-start = ((), (), s32[]{:S(2)}) async-start(), calls=%async_computation.4 | async-start | bytes 37748736 | tf_op jit(solution)/shard_map/psum | solution.py:397
  350.5 8.6 copy-start.71
  350.5 8.6 copy-start.120
  359.1 10.4 %copy-start.38 = (bf16[6,64,512]{2,1,0:T(8,128)(2,1)S(1)}, bf16[6,64,512]{2,1,0:T(8,128)(2,1)}, u32[]{:S(2)}) copy-start(bf16[6,64,512]{2,1,0:T(8,128)(2,1)} %copy-done.37) | copy-start | bytes 1179652
  359.1 10.4 %copy-start.55 = (bf16[1,512,768]{2,1,0:T(8,128)(2,1)S(1)}, bf16[1,512,768]{2,1,0:T(8,128)(2,1)}, u32[]{:S(2)}) copy-start(bf16[1,512,768]{2,1,0:T(8,128)(2,1)} %param.22) | copy-start | bytes 2359300
  386.5 19.0 %slice-start.14 = ((s8[6291456]{0:T(1024)(128)(4,1)}), s8[2097152]{0:T(1024)(128)(4,1)S(1)}, s32[]{:S(2)}) async-start(s8[6291456]{0:T(1024)(128)(4,1)} %bitcast.224), calls=%async_computation.20 | async-start | bytes 4194304
  387.1 18.3 %slice-start.15 = ((s8[6291456]{0:T(1024)(128)(4,1)}), s8[4194304]{0:T(1024)(128)(4,1)S(1)}, s32[]{:S(2)}) async-start(s8[6291456]{0:T(1024)(128)(4,1)} %bitcast.224), calls=%async_computation.21 | async-start | bytes 8388608
  387.1 18.3 %copy-start.64 = (s32[512,1024]{1,0:T(8,128)S(1)}, s32[512,1024]{1,0:T(8,128)}, u32[]{:S(2)}) copy-start(s32[512,1024]{1,0:T(8,128)} %copy-done.63) | copy-start | bytes 6291460
  425.3 85.2 %copy-start.10 = (f32[1024,768]{1,0:T(8,128)S(1)}, f32[1024,768]{1,0:T(8,128)}, u32[]{:S(2)}) copy-start(f32[1024,768]{1,0:T(8,128)} %copy-done.8) | copy-start | bytes 9437188
  425.3 88.7 %copy-start.123 = (f32[1024]{0:T(1024)S(1)}, f32[1024]{0:T(1024)}, u32[]{:S(2)}) copy-start(f32[1024]{0:T(1024)} %get-tuple-element.90) | copy-start | bytes 12292
  517.5 405.9 %copy-start.72 = (f32[1,512,768]{2,1,0:T(8,128)S(1)}, f32[1,512,768]{2,1,0:T(8,128)}, u32[]{:S(2)}) copy-start(f32[1,512,768]{2,1,0:T(8,128)} %get-tuple-element.118) | copy-start | bytes 4718596
  923.4 8.1 slice-start.18
  (113 other events, 338.3 us)
Sparse Core Ops, SparseCore 0:
  115.6 25.8 all-reduce.9
  158.0 24.3 all-reduce.11
  202.3 24.3 all-reduce.13
  256.5 24.3 all-reduce.15
  350.2 36.4 all-reduce.19
  395.9 522.0 all-reduce.17
where the time goes:
time: 953 us; the launch traced here: 944 us
  waiting for transfers between devices  473 us (50%)
  matrix products  264 us (28%)
  blocking collectives  81.4 us (9%)
  other arithmetic  66.1 us (7%)
  local copies, waits for them, and re-layouts  40.3 us (4%)
  between operations  18.3 us (2%)
    psum x1, waiting for transfers between devices, body(): lax.psum((grad_self_gain, grad_self_query, grad_self_key, grad_self_value...  400 us
    psum x1, blocking collectives, body(): lax.psum((grad_self_gain, grad_self_query, grad_self_key, grad_self_value...  81.4 us
    dot_general x2, matrix products, lookup_bias(): jnp.einsum('ptn,po->otn', one_hot_encoding.astype(jnp.float32), position_...  51.3 us
    unnamed x321, local copies, waits for them, and re-layouts  39.3 us
    dot_general x2, matrix products, attend_back(): jnp.einsum('dju,cju->cd', grad_scores, one_hot_encoding.astype(jnp.bfloat...  38.1 us
    dot_general x10, matrix products, left_contract(): jnp.einsum('ti,tj->ij', former, latter, preferred_element_type=jnp.float32)  34.9 us
    dot_general x4, matrix products, block_scores(): jnp.einsum('qhd,khd->hqk', split_heads(query_block, head_count), split_he...  33.1 us
    dot_general x10, matrix products, matrix_product(): return jnp.dot(former, latter, preferred_element_type=jnp.float32)  24.8 us
  transfers between devices with their start and end apart: 6, of which 5 were waited for; matrix products, arithmetic and copies ran while one was open for 11% of the time, Pallas kernels for 0%

commit v1 on v0

--- a/solution.py
+++ b/solution.py
@@ -226,6 +226,70 @@
                 preferred_element_type=jnp.float32,
             )
     return (jnp.concatenate(query_parts, axis=0), grad_key_rows, grad_value_rows, grad_table)
+
+
+def flip(array, axis_name, size, bit):
+    return lax.ppermute(array, axis_name, [(i, i ^ (1 << bit)) for i in range(size)])
+
+
+def core_sum(array):
+    size = lax.axis_size("tensor")
+    if size != 2:
+        return lax.psum(array, "tensor")
+    return array + lax.ppermute(array, "tensor", [(0, 1), (1, 0)])
+
+
+def bit_of(bit):
+    return (lax.axis_index("dp") >> bit) & 1
+
+
+def part_of(array, upper, axis):
+    half = array.shape[axis] // 2
+    return lax.dynamic_slice_in_dim(array, upper * half, half, axis)
+
+
+def halve(terms, bit, axis):
+    mine = bit_of(bit)
+    send = sum(part_of(t, 1 - mine, axis) for t in terms)
+    keep = sum(part_of(t, mine, axis) for t in terms)
+    return [keep, flip(send, "dp", lax.axis_size("dp"), bit)]
+
+
+def double(array, bit, axis):
+    other = flip(array, "dp", lax.axis_size("dp"), bit)
+    low = jnp.concatenate([array, other], axis=axis)
+    high = jnp.concatenate([other, array], axis=axis)
+    return jnp.where(bit_of(bit) == 0, low, high)
+
+
+def chunk_sum(chunk):
+    if lax.axis_size("dp") != 16:
+        return lax.psum(chunk, "dp")
+    rows = chunk.shape[0]
+    terms_a = halve([chunk[: rows // 2]], 0, 0)
+    terms_b = halve([chunk[rows // 2 :]], 1, 0)
+    terms_a = halve(terms_a, 1, 0)
+    terms_b = halve(terms_b, 0, 0)
+    terms = [jnp.stack([a, b]) for a, b in zip(terms_a, terms_b)]
+    terms = halve(terms, 2, 1)
+    terms = halve(terms, 3, 1)
+    own = terms[0] + terms[1]
+    own = double(own, 3, 1)
+    own = double(own, 2, 1)
+    a = double(own[0], 1, 0)
+    b = double(own[1], 0, 0)
+    a = double(a, 0, 0)
+    b = double(b, 1, 0)
+    return jnp.concatenate([a, b], axis=0)
+
+
+def small_sum(array):
+    size = lax.axis_size("dp")
+    if size != 16:
+        return lax.psum(array, "dp")
+    for bit in range(4):
+        array = array + flip(array, "dp", size, bit)
+    return array
 
 
 def body(
@@ -275,7 +339,7 @@
     mixed_parts.append(mixed)
     totals_one = [log_totals]
     mixed_one = mixed_parts[0]
-    self_branch = lax.psum(matrix_product(mixed_one, self_output), "tensor")
+    self_branch = core_sum(matrix_product(mixed_one, self_output))
     first = decoder_rows + self_branch
     second_normalized, rms_two = normalize(first, cross_gain)
     input_two = second_normalized.astype(jnp.bfloat16)
@@ -296,14 +360,14 @@
     mixed_parts.append(mixed)
     totals_two = [log_totals]
     mixed_two = mixed_parts[0]
-    cross_branch = lax.psum(matrix_product(mixed_two, cross_output), "tensor")
+    cross_branch = core_sum(matrix_product(mixed_two, cross_output))
     second = first + cross_branch
     normed_three, rms_three = normalize(second, hidden_gain)
     input_three = normed_three.astype(jnp.bfloat16)
     before = matrix_product(input_three, hidden_in)
     gelu_tanh = partial(jax.nn.gelu, approximate=True)
     active = gelu_tanh(before).astype(jnp.bfloat16)
-    hidden_branch = lax.psum(matrix_product(active, hidden_out), "tensor")
+    hidden_branch = core_sum(matrix_product(active, hidden_out))
     third = second + hidden_branch
     layer_out = third.astype(jnp.bfloat16).reshape(item_count, target, model_width)
     places = jnp.arange(target, dtype=jnp.int32)
@@ -319,11 +383,10 @@
     gelu_value, gelu_pull = jax.vjp(gelu_tanh, before)
     grad_before = gelu_pull(grad_active)[0].astype(jnp.bfloat16)
     grad_hidden_in = left_contract(input_three, grad_before)
-    grad_input_three = lax.psum(right_contract(grad_before, hidden_in), "tensor")
+    grad_input_three = core_sum(right_contract(grad_before, hidden_in))
     back_three, grad_hidden_gain = norm_back(second, rms_three, hidden_gain, grad_input_three)
     grad_second = grad_third + back_three
     grad_branch_two = grad_second.astype(jnp.bfloat16)
-    grad_cross_output = left_contract(mixed_two, grad_branch_two)
     grad_mixed_two = right_contract(grad_branch_two, cross_output).astype(jnp.bfloat16)
     query_parts = []
     key_parts = []
@@ -349,17 +412,13 @@
     grad_cross_query = left_contract(input_two, grad_queries_two)
     grad_cross_key = left_contract(encoder_rows, grad_keys_two)
     grad_cross_value = left_contract(encoder_rows, grad_values_two)
-    grad_input_two, grad_encoder = lax.psum(
-        (
-            right_contract(grad_queries_two, cross_query),
-            right_contract(grad_keys_two, cross_key) + right_contract(grad_values_two, cross_value),
-        ),
-        "tensor",
+    grad_input_two = core_sum(right_contract(grad_queries_two, cross_query))
+    grad_encoder = core_sum(
+        right_contract(grad_keys_two, cross_key) + right_contract(grad_values_two, cross_value)
     )
     back_two, grad_cross_gain = norm_back(first, rms_two, cross_gain, grad_input_two)
     grad_first = grad_second + back_two
     grad_branch_one = grad_first.astype(jnp.bfloat16)
-    grad_self_output = left_contract(mixed_one, grad_branch_one)
     grad_mixed_one = right_contract(grad_branch_one, self_output).astype(jnp.bfloat16)
     query_parts = []
     key_parts = []
@@ -385,52 +444,62 @@
     grad_self_query = left_contract(input_one, grad_queries_one)
     grad_self_key = left_contract(input_one, grad_keys_one)
     grad_self_value = left_contract(input_one, grad_values_one)
-    grad_input_one = lax.psum(
+    grad_input_one = core_sum(
         right_contract(grad_queries_one, self_query)
         + right_contract(grad_keys_one, self_attention_key)
-        + right_contract(grad_values_one, self_value),
-        "tensor",
+        + right_contract(grad_values_one, self_value)
     )
     back_one, grad_self_gain = norm_back(decoder_rows, rms_one, self_gain, grad_input_one)
     grad_decoder = (grad_first + back_one).reshape(item_count, target, model_width)
     grad_encoder = grad_encoder.reshape(item_count, source, model_width)
-    every_sum = lax.psum(
-        (
-            grad_self_gain,
+    width = self_query.shape[1]
+    cross_chunk = jnp.concatenate(
+        [
+            grad_cross_query,
+            grad_cross_key,
+            grad_cross_value,
+            left_contract(grad_branch_two, mixed_two),
+        ],
+        axis=1,
+    )
+    self_chunk = jnp.concatenate(
+        [
             grad_self_query,
             grad_self_key,
             grad_self_value,
-            grad_self_output,
-            grad_table,
-            grad_cross_gain,
-            grad_cross_query,
-            grad_cross_key,
-            grad_cross_value,
-            grad_cross_output,
-            grad_hidden_gain,
-            grad_hidden_in,
-            grad_hidden_out,
-        ),
-        "dp",
-    )
+            left_contract(grad_branch_one, mixed_one),
+        ],
+        axis=1,
+    )
+    sum_out = chunk_sum(grad_hidden_out)
+    sum_in = chunk_sum(grad_hidden_in)
+    sum_cross = chunk_sum(cross_chunk)
+    sum_self = chunk_sum(self_chunk)
+    pieces = [grad_self_gain, grad_cross_gain, grad_hidden_gain, grad_table.reshape(-1)]
+    flat = jnp.concatenate(pieces)
+    lanes = 512
+    flat = jnp.pad(flat, (0, -flat.shape[0] % (8 * lanes))).reshape(-1, lanes)
+    flat = small_sum(flat).reshape(-1)
+    gains = [flat[i * model_width : (i + 1) * model_width] for i in range(3)]
+    table = flat[3 * model_width : 3 * model_width + grad_table.size].reshape(grad_table.shape)
     return (
         layer_out,
         grad_decoder,
         grad_encoder,
-        every_sum[0],
-        every_sum[1],
-        every_sum[2],
-        every_sum[3],
-        every_sum[4],
-        every_sum[5],
-        every_sum[6],
-        every_sum[7],
-        every_sum[8],
-        every_sum[9],
-        every_sum[10],
-        every_sum[11],
-        every_sum[12],
-        every_sum[13],
+        gains[0],
+        sum_self[:, :width],
+        sum_self[:, width : 2 * width],
+        sum_self[:, 2 * width : 3 * width],
+        sum_self[:, 3 * width :].T,
+        table,
+        gains[1],
+        sum_cross[:, :width],
+        sum_cross[:, width : 2 * width],
+        sum_cross[:, 2 * width : 3 * width],
+        sum_cross[:, 3 * width :].T,
+        gains[2],
+        sum_in,
+        sum_out,
     )
 
 

time: 953 us -> 761 us (0.80)
  waiting for transfers between devices: 473 us -> 267 us
  blocking collectives: 81.4 us -> 0 us
  other arithmetic: 66.1 us -> 133 us
  starting transfers between devices: 1.64 us -> 66.9 us
  matrix products: 264 us -> 240 us
  between operations: 18.3 us -> 4.56 us
    psum x6 -> x0, waiting for transfers between devices: 473 us -> none  [the longest x1 400 us: body(): lax.psum((grad_self_gain, grad_self_query, grad_self_key, grad_self_value...]
    ppermute x0 -> x59, waiting for transfers between devices: none -> 267 us  [the longest x52 261 us: flip(): lax.ppermute(array, axis_name, [(i, i ^ 1 << bit) for i in range(size)])]
    psum x1 -> x0, blocking collectives: 81.4 us -> none  [body(): lax.psum((grad_self_gain, grad_self_query, grad_self_key, grad_self_value...]
    ppermute x0 -> x59, starting transfers between devices: none -> 66.9 us  [the longest x52 66 us: flip(): lax.ppermute(array, axis_name, [(i, i ^ 1 << bit) for i in range(size)])]
    select_n x0 -> x24, other arithmetic: none -> 33.2 us  [double(): return jnp.where(bit_of(bit) == 0, low, high)]
    dot_general x10, matrix products: 34.9 us -> 15.4 us  [left_contract(): jnp.einsum('ti,tj->ij', former, latter, preferred_element_type=jnp.float32)]
    unnamed x321 -> x260, local copies, waits for them, and re-layouts: 39.3 us -> 28 us
  transfers between devices with their start and end apart: 6 -> 59, of which waited for: 5 -> 31; matrix products, arithmetic and copies ran while one was open for 11% -> 35% of each run, Pallas kernels for 0% -> 0%
where the time goes in v1:
time: 761 us; the launch traced here: 752 us
  waiting for transfers between devices  267 us (35%)
  matrix products  240 us (32%)
  other arithmetic  133 us (17%)
  starting transfers between devices  66.9 us (9%)
  local copies, waits for them, and re-layouts  40.5 us (5%)
    ppermute x52, waiting for transfers between devices, flip(): lax.ppermute(array, axis_name, [(i, i ^ 1 << bit) for i in range(size)])  261 us
    ppermute x52, starting transfers between devices, flip(): lax.ppermute(array, axis_name, [(i, i ^ 1 << bit) for i in range(size)])  66 us
    dot_general x2, matrix products, lookup_bias(): jnp.einsum('ptn,po->otn', one_hot_encoding.astype(jnp.float32), position_...  51.3 us
    dot_general x2, matrix products, attend_back(): jnp.einsum('dju,cju->cd', grad_scores, one_hot_encoding.astype(jnp.bfloat...  39.6 us
    select_n x24, other arithmetic, double(): return jnp.where(bit_of(bit) == 0, low, high)  33.2 us
    dot_general x4, matrix products, block_scores(): jnp.einsum('qhd,khd->hqk', split_heads(query_block, head_count), split_he...  32.9 us
    unnamed x260, local copies, waits for them, and re-layouts  28 us
    convert_element_type x3, other arithmetic, backward_block(): grad_scores = (shares * (grad_shares - inner_sum)).astype(jnp.bfloat16)  26.4 us
  transfers between devices with their start and end apart: 59, of which 31 were waited for; matrix products, arithmetic and copies ran while one was open for 35% of the time, Pallas kernels for 0%

profile of v1, /device:TPU:0, one launch (start us, length us, event | category | flops | bytes accessed | tf_op | source)
XLA Modules:
  0.0 752.4 jit_solution(2477188387244108328)
XLA Ops:
  13.8 25.6 %fusion.3 = f32[512,1024,6]{1,2,0:T(8,128)} fusion(s32[512,1024]{1,0:T(8,128)S(1)} %subtract_clamp_fusion, s32[32]{0:T(128)S(1)} %get-tuple-element.188, s32[32]{0:T(128)S(1)} %get-tuple-element.187, f32[32,6]{0,1:T(8,128)S(1)} %copy-done.109), kind=kOutput, calls=%fused_computation.5 | convolution fusion | flops 1258291200 | bytes 14681088 | tf_op jit(solution)/shard_map/ptn,po->otn/dot_general | solution.py:50
  39.3 25.7 %fusion.1 = f32[512,1024,6]{1,2,0:T(8,128)} fusion(s32[512,1024]{1,0:T(8,128)S(1)} %copy-done.62, s32[32]{0:T(128)S(1)} %get-tuple-element.188, s32[32]{0:T(128)S(1)} %get-tuple-element.187, f32[32,6]{0,1:T(8,128)S(1)} %copy-done.109), kind=kOutput, calls=%fused_computation.3 | convolution fusion | flops 1258291200 | bytes 14681088 | tf_op jit(solution)/shard_map/ptn,po->otn/dot_general | solution.py:50
  65.1 14.5 %fusion.185 = (f32[6,512]{1,0:T(8,128)S(1)}, f32[6,512,1024]{2,1,0:T(8,128)S(1)}) fusion(f32[512,1024,6]{1,2,0:T(8,128)} %fusion.3, bf16[512,6,64]{0,2,1:T(8,128)(2,1)S(1)} %bitcast.279, bf16[1024,6,64]{0,2,1:T(8,128)(2,1)S(1)} %bitcast.271, pred[512,1024]{1,0:T(8,128)(4,1)S(1)} %get-tuple-element.184), kind=kOutput, calls=%fused_computation.373 | convolution fusion | flops 412087296 | bytes 26882048 | tf_op jit(solution)/shard_map/qhd,khd->hqk/dot_general | solution.py:82
  87.5 14.7 %fusion.186 = (f32[6,512]{1,0:T(8,128)S(1)}, f32[6,512,1024]{2,1,0:T(8,128)S(1)}) fusion(f32[512,1024,6]{1,2,0:T(8,128)} %fusion.1, bf16[512,6,64]{0,2,1:T(8,128)(2,1)S(1)} %bitcast.281, bf16[1024,6,64]{0,2,1:T(8,128)(2,1)S(1)} %bitcast.272, pred[512,1024]{1,0:T(8,128)(4,1)S(1)} %get-tuple-element.183), kind=kOutput, calls=%fused_computation.374 | convolution fusion | flops 412087296 | bytes 26882048 | tf_op jit(solution)/shard_map/qhd,khd->hqk/dot_general | solution.py:82
  114.3 3.5 collective-permute-done
  137.5 5.0 multiply_reduce_fusion.8
  145.4 4.4 fusion.79
  156.7 6.8 fusion.30
  170.1 6.3 fusion.187
  176.4 4.8 collective-permute-done.47
  187.7 21.9 %collective-permute-done.36 = f32[192,1536]{1,0:T(8,128)} collective-permute-done((f32[192,1536]{1,0:T(8,128)}, f32[192,1536]{1,0:T(8,128)}, u32[]{:S(2)}, u32[]{:S(2)}) %collective-permute-start.36) | collective-permute-done | bytes 1179680 | tf_op jit(solution)/shard_map/ppermute | solution.py:232
  214.8 7.5 fusion.169
  224.8 6.3 collective-permute-done.38
  242.3 16.0 %collective-permute-done.39 = f32[2,48,1536]{2,1,0:T(8,128)} collective-permute-done((f32[2,48,1536]{2,1,0:T(8,128)}, f32[2,48,1536]{2,1,0:T(8,128)}, u32[]{:S(2)}, u32[]{:S(2)}) %collective-permute-start.39) | collective-permute-done | bytes 589856 | tf_op jit(solution)/shard_map/ppermute | solution.py:232
  263.4 19.3 %collective-permute-done.40 = f32[2,24,1536]{2,1,0:T(8,128)} collective-permute-done((f32[2,24,1536]{2,1,0:T(8,128)S(1)}, f32[2,24,1536]{2,1,0:T(8,128)}, u32[]{:S(2)}, u32[]{:S(2)}) %collective-permute-start.40) | collective-permute-done | bytes 294944 | tf_op jit(solution)/shard_map/ppermute | solution.py:232
  283.9 11.3 %collective-permute-done.53 = f32[2,48,768]{2,1,0:T(8,128)S(1)} collective-permute-done((f32[2,48,768]{2,1,0:T(8,128)S(1)}, f32[2,48,768]{2,1,0:T(8,128)S(1)}, u32[]{:S(2)}, u32[]{:S(2)}) %collective-permute-start.53) | collective-permute-done | bytes 294944 | tf_op jit(solution)/shard_map/ppermute | solution.py:232
  296.1 4.5 collective-permute-done.41
  301.4 5.5 multiply_reduce_fusion.4
  306.9 6.9 bitcast_add_fusion.2
  322.5 5.2 multiply_reduce_fusion.3
  327.7 8.1 %multiply_convert_fusion.3 = (bf16[6,512,512]{1,2,0:T(8,128)(2,1)}, bf16[6,512,512]{1,2,0:T(8,128)(2,1)S(1)}) fusion(f32[6,512,512]{1,2,0:T(8,128)} %get-tuple-element.196, f32[6,512,512]{1,2,0:T(8,128)S(1)} %bitcast.264, f32[6,512]{1,0:T(8,128)S(1)} %get-tuple-element.108, f32[6,512]{1,0:T(8,128)S(1)} %get-tuple-element.202, ...), kind=kLoop, calls=%fused_computation.66 | loop fusion | flops 15728640 | bytes 31506944 | tf_op jit(solution)/shard_map/convert_element_type | solution.py:125
  366.1 23.4 %collective-permute-done.55 = f32[192,768]{1,0:T(8,128)} collective-permute-done((f32[192,768]{1,0:T(8,128)}, f32[192,768]{1,0:T(8,128)}, u32[]{:S(2)}, u32[]{:S(2)}) %collective-permute-start.55) | collective-permute-done | bytes 589856 | tf_op jit(solution)/shard_map/ppermute | solution.py:232
  392.7 7.9 %collective-permute-done.43 = f32[96,1536]{1,0:T(8,128)} collective-permute-done((f32[96,1536]{1,0:T(8,128)}, f32[96,1536]{1,0:T(8,128)}, u32[]{:S(2)}, u32[]{:S(2)}) %collective-permute-start.43) | collective-permute-done | bytes 589856 | tf_op jit(solution)/shard_map/ppermute | solution.py:232
  409.9 7.0 collective-permute-done.45
  419.0 35.8 %collective-permute-done.26 = f32[96,1536]{1,0:T(8,128)S(1)} collective-permute-done((f32[96,1536]{1,0:T(8,128)S(1)}, f32[96,1536]{1,0:T(8,128)S(1)}, u32[]{:S(2)}, u32[]{:S(2)}) %collective-permute-start.26) | collective-permute-done | bytes 589856 | tf_op jit(solution)/shard_map/ppermute | solution.py:232
  461.4 16.3 %collective-permute-done.56 = f32[384,768]{1,0:T(8,128)S(1)} collective-permute-done((f32[384,768]{1,0:T(8,128)S(1)}, f32[384,768]{1,0:T(8,128)S(1)}, u32[]{:S(2)}, u32[]{:S(2)}) %collective-permute-start.56) | collective-permute-done | bytes 1179680 | tf_op jit(solution)/shard_map/ppermute | solution.py:232
  486.6 8.8 %collective-permute-done.28 = f32[2,24,1536]{2,1,0:T(8,128)S(1)} collective-permute-done((f32[2,24,1536]{2,1,0:T(8,128)S(1)}, f32[2,24,1536]{2,1,0:T(8,128)S(1)}, u32[]{:S(2)}, u32[]{:S(2)}) %collective-permute-start.28) | collective-permute-done | bytes 294944 | tf_op jit(solution)/shard_map/ppermute | solution.py:232
  498.0 13.0 %collective-permute-done.29 = f32[2,24,1536]{2,1,0:T(8,128)S(1)} collective-permute-done((f32[2,24,1536]{2,1,0:T(8,128)S(1)}, f32[2,24,1536]{2,1,0:T(8,128)S(1)}, u32[]{:S(2)}, u32[]{:S(2)}) %collective-permute-start.29) | collective-permute-done | bytes 294944 | tf_op jit(solution)/shard_map/ppermute | solution.py:232
  522.7 6.6 multiply_reduce_fusion
  532.5 6.2 multiply_reduce_fusion.1
  538.8 9.2 %multiply_convert_fusion.1 = bf16[6,512,1024]{2,1,0:T(8,128)(2,1)} fusion(f32[6,512,1024]{2,1,0:T(8,128)} %get-tuple-element.200, f32[6,512,1024]{2,1,0:T(8,128)S(1)} %bitcast.260, f32[6,512]{1,0:T(8,128)S(1)} %get-tuple-element.199, f32[6,512]{1,0:T(8,128)S(1)} %log_add_fusion.1), kind=kLoop, calls=%fused_computation.25 | loop fusion | flops 12582912 | bytes 31481856 | tf_op jit(solution)/shard_map/convert_element_type | solution.py:125
  548.0 5.0 convolution_convert_fusion.7
  555.4 9.1 %multiply_convert_fusion = bf16[6,512,1024]{2,1,0:T(8,128)(2,1)} fusion(f32[6,512,1024]{2,1,0:T(8,128)} %get-tuple-element.198, f32[6,512,1024]{2,1,0:T(8,128)S(1)} %bitcast.262, f32[6,512]{1,0:T(8,128)S(1)} %get-tuple-element.197, f32[6,512]{1,0:T(8,128)S(1)} %log_add_fusion), kind=kLoop, calls=%fused_computation.22 | loop fusion | flops 12582912 | bytes 31481856 | tf_op jit(solution)/shard_map/convert_element_type | solution.py:125
  564.4 5.0 convolution_convert_fusion.6
  580.4 19.6 %fusion.100 = f32[32,6]{0,1:T(8,128)S(1)} fusion(bf16[6,512,1024]{2,1,0:T(8,128)(2,1)S(1)} %bitcast.270, s32[512,1024]{1,0:T(8,128)S(1)} %copy-done.61, s32[32]{0:T(128)S(1)} %copy-done.106, s32[32]{0:T(128)S(1)} %copy-done.104), kind=kOutput, calls=%fused_computation.229 | convolution fusion | flops 251658240 | bytes 8389632 | tf_op jit(solution)/shard_map/dju,cju->cd/dot_general | solution.py:222
  600.0 5.4 collective-permute-done.12
  610.4 9.4 %collective-permute-done.14 = f32[96,1536]{1,0:T(8,128)S(1)} collective-permute-done((f32[96,1536]{1,0:T(8,128)S(1)}, f32[96,1536]{1,0:T(8,128)S(1)}, u32[]{:S(2)}, u32[]{:S(2)}) %collective-permute-start.14) | collective-permute-done | bytes 589856 | tf_op jit(solution)/shard_map/ppermute | solution.py:232
  624.4 9.6 %collective-permute-done.15 = f32[2,48,1536]{2,1,0:T(8,128)S(1)} collective-permute-done((f32[2,48,1536]{2,1,0:T(8,128)S(1)}, f32[2,48,1536]{2,1,0:T(8,128)S(1)}, u32[]{:S(2)}, u32[]{:S(2)}) %collective-permute-start.15) | collective-permute-done | bytes 589856 | tf_op jit(solution)/shard_map/ppermute | solution.py:232
  641.7 5.0 collective-permute-done.16
  647.5 20.0 %fusion.106 = f32[32,6]{0,1:T(8,128)S(1)} fusion(f32[32,6]{0,1:T(8,128)S(1)} %fusion.100, bf16[6,512,1024]{2,1,0:T(8,128)(2,1)S(1)} %bitcast.268, s32[512,1024]{1,0:T(8,128)S(1)} %copy-done.63, s32[32]{0:T(128)S(1)} %copy-done.106, s32[32]{0:T(128)S(1)} %copy-done.104), kind=kOutput, calls=%fused_computation.231 | convolution fusion | flops 251658432 | bytes 8390400 | tf_op jit(solution)/shard_map/dju,cju->cd/dot_general | solution.py:222
  675.2 4.5 collective-permute-done.32
  679.7 4.3 maximum_select_fusion.2
  684.0 4.1 fusion.58
  692.6 5.6 collective-permute-done.34
  708.8 4.1 collective-permute-start.9
  722.5 5.3 fusion.55
  727.9 3.5 copy.271
  732.8 9.6 %collective-permute-done.20 = f32[192,1536]{1,0:T(8,128)} collective-permute-done((f32[192,1536]{1,0:T(8,128)S(1)}, f32[192,1536]{1,0:T(8,128)}, u32[]{:S(2)}, u32[]{:S(2)}) %collective-permute-start.20) | collective-permute-done | bytes 1179680 | tf_op jit(solution)/shard_map/ppermute | solution.py:232
  (509 shorter events, 261.1 us)
Async XLA Ops:
  151.2 29.9 %collective-permute-start.47 = (f32[384,768]{1,0:T(8,128)}, f32[384,768]{1,0:T(8,128)}, u32[]{:S(2)}, u32[]{:S(2)}) collective-permute-start(f32[384,768]{1,0:T(8,128)} %constant_dynamic-slice_fusion), channel_id=1, source_target_pairs={{0,2},{2,0},{4,6},{6,4},{8,10},{10,8},{12,14},{14,12},{16,18},{18,... | collective-permute-start | bytes 3538952 | tf_op jit(solution)/shard_map/ppermute | solution.py:232
  155.2 29.6 %collective-permute-start.48 = (f32[384,768]{1,0:T(8,128)}, f32[384,768]{1,0:T(8,128)}, u32[]{:S(2)}, u32[]{:S(2)}) collective-permute-start(f32[384,768]{1,0:T(8,128)} %constant_dynamic-slice_fusion.5), channel_id=1, source_target_pairs={{0,4},{2,6},{4,0},{6,2},{8,12},{10,14},{12,8},{14,10},{16,20},{18,... | collective-permute-start | bytes 3538952 | tf_op jit(solution)/shard_map/ppermute | solution.py:232
  167.8 41.9 %collective-permute-start.36 = (f32[192,1536]{1,0:T(8,128)}, f32[192,1536]{1,0:T(8,128)}, u32[]{:S(2)}, u32[]{:S(2)}) collective-permute-start(f32[192,1536]{1,0:T(8,128)} %constant_dynamic-slice_fusion.1), channel_id=1, source_target_pairs={{0,4},{2,6},{4,0},{6,2},{8,12},{10,14},{12,8},{14,10},{16,20},{18,... | collective-permute-start | bytes 3538952 | tf_op jit(solution)/shard_map/ppermute | solution.py:232
  169.4 42.3 %collective-permute-start.35 = (f32[192,1536]{1,0:T(8,128)}, f32[192,1536]{1,0:T(8,128)}, u32[]{:S(2)}, u32[]{:S(2)}) collective-permute-start(f32[192,1536]{1,0:T(8,128)} %constant_dynamic-slice_fusion.2), channel_id=1, source_target_pairs={{0,2},{2,0},{4,6},{6,4},{8,10},{10,8},{12,14},{14,12},{16,18},{18,... | collective-permute-start | bytes 3538952 | tf_op jit(solution)/shard_map/ppermute | solution.py:232
  176.4 125.1 %collective-permute-start.3 = (f32[1024,768]{0,1:T(8,128)}, f32[1024,768]{0,1:T(8,128)}, u32[]{:S(2)}, u32[]{:S(2)}) collective-permute-start(f32[1024,768]{0,1:T(8,128)} %fusion.187), channel_id=1, source_target_pairs={{0,1},{1,0},{2,3},{3,2},{4,5},{5,4},{6,7},{7,6},{8,9},{9,8},{10,11... | collective-permute-start | bytes 9437192 | tf_op jit(solution)/shard_map/ppermute | solution.py:239
  182.6 39.7 %collective-permute-start.49 = (f32[192,768]{1,0:T(8,128)S(1)}, f32[192,768]{1,0:T(8,128)S(1)}, u32[]{:S(2)}, u32[]{:S(2)}) collective-permute-start(f32[192,768]{1,0:T(8,128)S(1)} %get-tuple-element.135), channel_id=1, source_target_pairs={{0,4},{2,6},{4,0},{6,2},{8,12},{10,14},{12,8},{14,10},{16,20},{18,... | collective-permute-start | bytes 1769480 | tf_op jit(solution)/shard_map/ppermute | solution.py:232
  186.2 36.1 %collective-permute-start.50 = (f32[192,768]{1,0:T(8,128)S(1)}, f32[192,768]{1,0:T(8,128)S(1)}, u32[]{:S(2)}, u32[]{:S(2)}) collective-permute-start(f32[192,768]{1,0:T(8,128)S(1)} %get-tuple-element.133), channel_id=1, source_target_pairs={{0,2},{2,0},{4,6},{6,4},{8,10},{10,8},{12,14},{14,12},{16,18},{18,... | collective-permute-start | bytes 1769480 | tf_op jit(solution)/shard_map/ppermute | solution.py:232
  211.1 20.0 %collective-permute-start.38 = (f32[96,1536]{1,0:T(8,128)S(1)}, f32[96,1536]{1,0:T(8,128)S(1)}, u32[]{:S(2)}, u32[]{:S(2)}) collective-permute-start(f32[96,1536]{1,0:T(8,128)S(1)} %get-tuple-element.137), channel_id=1, source_target_pairs={{0,2},{2,0},{4,6},{6,4},{8,10},{10,8},{12,14},{14,12},{16,18},{18,... | collective-permute-start | bytes 1769480 | tf_op jit(solution)/shard_map/ppermute | solution.py:232
  213.2 20.5 %collective-permute-start.37 = (f32[96,1536]{1,0:T(8,128)S(1)}, f32[96,1536]{1,0:T(8,128)S(1)}, u32[]{:S(2)}, u32[]{:S(2)}) collective-permute-start(f32[96,1536]{1,0:T(8,128)S(1)} %get-tuple-element.139), channel_id=1, source_target_pairs={{0,4},{2,6},{4,0},{6,2},{8,12},{10,14},{12,8},{14,10},{16,20},{18,... | collective-permute-start | bytes 1769480 | tf_op jit(solution)/shard_map/ppermute | solution.py:232
  222.3 84.7 %collective-permute-start.2 = (f32[1024,768]{0,1:T(8,128)}, f32[1024,768]{0,1:T(8,128)}, u32[]{:S(2)}, u32[]{:S(2)}) collective-permute-start(f32[1024,768]{0,1:T(8,128)} %fusion.169), channel_id=1, source_target_pairs={{0,1},{1,0},{2,3},{3,2},{4,5},{5,4},{6,7},{7,6},{8,9},{9,8},{10,11... | collective-permute-start | bytes 9437192 | tf_op jit(solution)/shard_map/ppermute | solution.py:239
  223.2 16.3 %collective-permute-start.51 = (f32[2,96,768]{2,1,0:T(8,128)}, f32[2,96,768]{2,1,0:T(8,128)S(1)}, u32[]{:S(2)}, u32[]{:S(2)}) collective-permute-start(f32[2,96,768]{2,1,0:T(8,128)} %get-tuple-element.151), channel_id=1, source_target_pairs={{0,8},{2,10},{4,12},{6,14},{8,0},{10,2},{12,4},{14,6},{16,24},{18,... | collective-permute-start | bytes 1769480 | tf_op jit(solution)/shard_map/ppermute | solution.py:232
  234.6 23.6 %collective-permute-start.39 = (f32[2,48,1536]{2,1,0:T(8,128)}, f32[2,48,1536]{2,1,0:T(8,128)}, u32[]{:S(2)}, u32[]{:S(2)}) collective-permute-start(f32[2,48,1536]{2,1,0:T(8,128)} %get-tuple-element.153), channel_id=1, source_target_pairs={{0,8},{2,10},{4,12},{6,14},{8,0},{10,2},{12,4},{14,6},{16,24},{18,... | collective-permute-start | bytes 1769480 | tf_op jit(solution)/shard_map/ppermute | solution.py:232
  239.6 21.4 %collective-permute-start.52 = (f32[2,48,768]{2,1,0:T(8,128)S(1)}, f32[2,48,768]{2,1,0:T(8,128)}, u32[]{:S(2)}, u32[]{:S(2)}) collective-permute-start(f32[2,48,768]{2,1,0:T(8,128)S(1)} %dynamic-slice_add_fusion.8), channel_id=1, source_target_pairs={{0,16},{2,18},{4,20},{6,22},{8,24},{10,26},{12,28},{14,30},{16,0},... | collective-permute-start | bytes 884744 | tf_op jit(solution)/shard_map/ppermute | solution.py:232
  259.2 23.4 %collective-permute-start.40 = (f32[2,24,1536]{2,1,0:T(8,128)S(1)}, f32[2,24,1536]{2,1,0:T(8,128)}, u32[]{:S(2)}, u32[]{:S(2)}) collective-permute-start(f32[2,24,1536]{2,1,0:T(8,128)S(1)} %dynamic-slice_add_fusion.9), channel_id=1, source_target_pairs={{0,16},{2,18},{4,20},{6,22},{8,24},{10,26},{12,28},{14,30},{16,0},... | collective-permute-start | bytes 884744 | tf_op jit(solution)/shard_map/ppermute | solution.py:232
  262.1 33.2 %collective-permute-start.53 = (f32[2,48,768]{2,1,0:T(8,128)S(1)}, f32[2,48,768]{2,1,0:T(8,128)S(1)}, u32[]{:S(2)}, u32[]{:S(2)}) collective-permute-start(f32[2,48,768]{2,1,0:T(8,128)S(1)} %add_add_fusion.2), channel_id=1, source_target_pairs={{0,16},{2,18},{4,20},{6,22},{8,24},{10,26},{12,28},{14,30},{16,0},... | collective-permute-start | bytes 884744 | tf_op jit(solution)/shard_map/ppermute | solution.py:232
  283.8 16.8 %collective-permute-start.41 = (f32[2,24,1536]{2,1,0:T(8,128)S(1)}, f32[2,24,1536]{2,1,0:T(8,128)S(1)}, u32[]{:S(2)}, u32[]{:S(2)}) collective-permute-start(f32[2,24,1536]{2,1,0:T(8,128)S(1)} %add_add_fusion.3), channel_id=1, source_target_pairs={{0,16},{2,18},{4,20},{6,22},{8,24},{10,26},{12,28},{14,30},{16,0},... | collective-permute-start | bytes 884744 | tf_op jit(solution)/shard_map/ppermute | solution.py:232
  296.1 57.0 %collective-permute-start.54 = (f32[2,96,768]{2,1,0:T(8,128)}, f32[2,96,768]{2,1,0:T(8,128)}, u32[]{:S(2)}, u32[]{:S(2)}) collective-permute-start(f32[2,96,768]{2,1,0:T(8,128)} %maximum_select_fusion.23), channel_id=1, source_target_pairs={{0,8},{2,10},{4,12},{6,14},{8,0},{10,2},{12,4},{14,6},{16,24},{18,... | collective-permute-start | bytes 1769480 | tf_op jit(solution)/shard_map/ppermute | solution.py:232
  301.4 56.0 %collective-permute-start.42 = (f32[2,48,1536]{2,1,0:T(8,128)}, f32[2,48,1536]{2,1,0:T(8,128)}, u32[]{:S(2)}, u32[]{:S(2)}) collective-permute-start(f32[2,48,1536]{2,1,0:T(8,128)} %maximum_select_fusion.22), channel_id=1, source_target_pairs={{0,8},{2,10},{4,12},{6,14},{8,0},{10,2},{12,4},{14,6},{16,24},{18,... | collective-permute-start | bytes 1769480 | tf_op jit(solution)/shard_map/ppermute | solution.py:232
  347.6 56.5 %collective-permute-start.24 = (f32[192,1536]{1,0:T(8,128)}, f32[192,1536]{1,0:T(8,128)}, u32[]{:S(2)}, u32[]{:S(2)}) collective-permute-start(f32[192,1536]{1,0:T(8,128)} %constant_dynamic-slice_fusion.3), channel_id=1, source_target_pairs={{0,4},{2,6},{4,0},{6,2},{8,12},{10,14},{12,8},{14,10},{16,20},{18,... | collective-permute-start | bytes 3538952 | tf_op jit(solution)/shard_map/ppermute | solution.py:232
  350.1 57.7 %collective-permute-start.23 = (f32[192,1536]{1,0:T(8,128)}, f32[192,1536]{1,0:T(8,128)}, u32[]{:S(2)}, u32[]{:S(2)}) collective-permute-start(f32[192,1536]{1,0:T(8,128)} %constant_dynamic-slice_fusion.4), channel_id=1, source_target_pairs={{0,2},{2,0},{4,6},{6,4},{8,10},{10,8},{12,14},{14,12},{16,18},{18,... | collective-permute-start | bytes 3538952 | tf_op jit(solution)/shard_map/ppermute | solution.py:232
  353.1 65.2 %collective-permute-start.6 = (f32[512,768]{1,0:T(8,128)}, f32[512,768]{1,0:T(8,128)}, u32[]{:S(2)}, u32[]{:S(2)}) collective-permute-start(f32[512,768]{1,0:T(8,128)} %convolution_add_fusion), channel_id=1, source_target_pairs={{0,1},{1,0},{2,3},{3,2},{4,5},{5,4},{6,7},{7,6},{8,9},{9,8},{10,11... | collective-permute-start | bytes 4718600 | tf_op jit(solution)/shard_map/ppermute | solution.py:239
  356.0 33.5 %collective-permute-start.55 = (f32[192,768]{1,0:T(8,128)}, f32[192,768]{1,0:T(8,128)}, u32[]{:S(2)}, u32[]{:S(2)}) collective-permute-start(f32[192,768]{1,0:T(8,128)} %get-tuple-element.158), channel_id=1, source_target_pairs={{0,4},{2,6},{4,0},{6,2},{8,12},{10,14},{12,8},{14,10},{16,20},{18,... | collective-permute-start | bytes 1769480 | tf_op jit(solution)/shard_map/ppermute | solution.py:232
  360.3 40.3 %collective-permute-start.43 = (f32[96,1536]{1,0:T(8,128)}, f32[96,1536]{1,0:T(8,128)}, u32[]{:S(2)}, u32[]{:S(2)}) collective-permute-start(f32[96,1536]{1,0:T(8,128)} %get-tuple-element.160), channel_id=1, source_target_pairs={{0,4},{2,6},{4,0},{6,2},{8,12},{10,14},{12,8},{14,10},{16,20},{18,... | collective-permute-start | bytes 1769480 | tf_op jit(solution)/shard_map/ppermute | solution.py:232
  389.5 16.7 %collective-permute-start.57 = (f32[192,768]{1,0:T(8,128)S(1)}, f32[192,768]{1,0:T(8,128)S(1)}, u32[]{:S(2)}, u32[]{:S(2)}) collective-permute-start(f32[192,768]{1,0:T(8,128)S(1)} %copy-done.59), channel_id=1, source_target_pairs={{0,2},{2,0},{4,6},{6,4},{8,10},{10,8},{12,14},{14,12},{16,18},{18,... | collective-permute-start | bytes 1769480 | tf_op jit(solution)/shard_map/ppermute | solution.py:232
  400.6 16.3 %collective-permute-start.45 = (f32[96,1536]{1,0:T(8,128)S(1)}, f32[96,1536]{1,0:T(8,128)S(1)}, u32[]{:S(2)}, u32[]{:S(2)}) collective-permute-start(f32[96,1536]{1,0:T(8,128)S(1)} %copy-done.58), channel_id=1, source_target_pairs={{0,2},{2,0},{4,6},{6,4},{8,10},{10,8},{12,14},{14,12},{16,18},{18,... | collective-permute-start | bytes 1769480 | tf_op jit(solution)/shard_map/ppermute | solution.py:232
  404.1 55.5 %collective-permute-start.44 = (f32[192,1536]{1,0:T(8,128)S(1)}, f32[192,1536]{1,0:T(8,128)S(1)}, u32[]{:S(2)}, u32[]{:S(2)}) collective-permute-start(f32[192,1536]{1,0:T(8,128)S(1)} %maximum_select_fusion.15), channel_id=1, source_target_pairs={{0,2},{2,0},{4,6},{6,4},{8,10},{10,8},{12,14},{14,12},{16,18},{18,... | collective-permute-start | bytes 3538952 | tf_op jit(solution)/shard_map/ppermute | solution.py:232
  406.2 48.6 %collective-permute-start.26 = (f32[96,1536]{1,0:T(8,128)S(1)}, f32[96,1536]{1,0:T(8,128)S(1)}, u32[]{:S(2)}, u32[]{:S(2)}) collective-permute-start(f32[96,1536]{1,0:T(8,128)S(1)} %get-tuple-element.141), channel_id=1, source_target_pairs={{0,2},{2,0},{4,6},{6,4},{8,10},{10,8},{12,14},{14,12},{16,18},{18,... | collective-permute-start | bytes 1769480 | tf_op jit(solution)/shard_map/ppermute | solution.py:232
  407.8 69.8 %collective-permute-start.56 = (f32[384,768]{1,0:T(8,128)S(1)}, f32[384,768]{1,0:T(8,128)S(1)}, u32[]{:S(2)}, u32[]{:S(2)}) collective-permute-start(f32[384,768]{1,0:T(8,128)S(1)} %maximum_select_fusion.18), channel_id=1, source_target_pairs={{0,2},{2,0},{4,6},{6,4},{8,10},{10,8},{12,14},{14,12},{16,18},{18,... | collective-permute-start | bytes 3538952 | tf_op jit(solution)/shard_map/ppermute | solution.py:232
  416.9 61.0 %collective-permute-start.58 = (f32[384,768]{1,0:T(8,128)S(1)}, f32[384,768]{1,0:T(8,128)S(1)}, u32[]{:S(2)}, u32[]{:S(2)}) collective-permute-start(f32[384,768]{1,0:T(8,128)S(1)} %maximum_select_fusion.19), channel_id=1, source_target_pairs={{0,4},{2,6},{4,0},{6,2},{8,12},{10,14},{12,8},{14,10},{16,20},{18,... | collective-permute-start | bytes 3538952 | tf_op jit(solution)/shard_map/ppermute | solution.py:232
  418.3 39.7 %collective-permute-start.25 = (f32[96,1536]{1,0:T(8,128)S(1)}, f32[96,1536]{1,0:T(8,128)S(1)}, u32[]{:S(2)}, u32[]{:S(2)}) collective-permute-start(f32[96,1536]{1,0:T(8,128)S(1)} %get-tuple-element.143), channel_id=1, source_target_pairs={{0,4},{2,6},{4,0},{6,2},{8,12},{10,14},{12,8},{14,10},{16,20},{18,... | collective-permute-start | bytes 1769480 | tf_op jit(solution)/shard_map/ppermute | solution.py:232
  454.8 57.1 %collective-permute-start.4 = (f32[1024,768]{0,1:T(8,128)S(1)}, f32[1024,768]{0,1:T(8,128)S(1)}, u32[]{:S(2)}, u32[]{:S(2)}) collective-permute-start(f32[1024,768]{0,1:T(8,128)S(1)} %fusion.146), channel_id=1, source_target_pairs={{0,1},{1,0},{2,3},{3,2},{4,5},{5,4},{6,7},{7,6},{8,9},{9,8},{10,11... | collective-permute-start | bytes 9437192 | tf_op jit(solution)/shard_map/ppermute | solution.py:239
  458.0 28.4 %collective-permute-start.46 = (f32[192,1536]{1,0:T(8,128)S(1)}, f32[192,1536]{1,0:T(8,128)S(1)}, u32[]{:S(2)}, u32[]{:S(2)}) collective-permute-start(f32[192,1536]{1,0:T(8,128)S(1)} %maximum_select_fusion.16), channel_id=1, source_target_pairs={{0,4},{2,6},{4,0},{6,2},{8,12},{10,14},{12,8},{14,10},{16,20},{18,... | collective-permute-start | bytes 3538952 | tf_op jit(solution)/shard_map/ppermute | solution.py:232
  459.6 21.0 %collective-permute-start.27 = (f32[2,48,1536]{2,1,0:T(8,128)S(1)}, f32[2,48,1536]{2,1,0:T(8,128)S(1)}, u32[]{:S(2)}, u32[]{:S(2)}) collective-permute-start(f32[2,48,1536]{2,1,0:T(8,128)S(1)} %get-tuple-element.155), channel_id=1, source_target_pairs={{0,8},{2,10},{4,12},{6,14},{8,0},{10,2},{12,4},{14,6},{16,24},{18,... | collective-permute-start | bytes 1769480 | tf_op jit(solution)/shard_map/ppermute | solution.py:232
  511.9 109.5 %collective-permute-start.30 = (f32[2,48,1536]{2,1,0:T(8,128)}, f32[2,48,1536]{2,1,0:T(8,128)}, u32[]{:S(2)}, u32[]{:S(2)}) collective-permute-start(f32[2,48,1536]{2,1,0:T(8,128)} %maximum_select_fusion.21), channel_id=1, source_target_pairs={{0,8},{2,10},{4,12},{6,14},{8,0},{10,2},{12,4},{14,6},{16,24},{18,... | collective-permute-start | bytes 1769480 | tf_op jit(solution)/shard_map/ppermute | solution.py:232
  578.0 27.4 %collective-permute-start.12 = (f32[192,1536]{1,0:T(8,128)S(1)}, f32[192,1536]{1,0:T(8,128)S(1)}, u32[]{:S(2)}, u32[]{:S(2)}) collective-permute-start(f32[192,1536]{1,0:T(8,128)S(1)} %constant_dynamic-slice_fusion.6), channel_id=1, source_target_pairs={{0,4},{2,6},{4,0},{6,2},{8,12},{10,14},{12,8},{14,10},{16,20},{18,... | collective-permute-start | bytes 3538952 | tf_op jit(solution)/shard_map/ppermute | solution.py:232
  579.8 27.4 %collective-permute-start.11 = (f32[192,1536]{1,0:T(8,128)S(1)}, f32[192,1536]{1,0:T(8,128)S(1)}, u32[]{:S(2)}, u32[]{:S(2)}) collective-permute-start(f32[192,1536]{1,0:T(8,128)S(1)} %constant_dynamic-slice_fusion.7), channel_id=1, source_target_pairs={{0,2},{2,0},{4,6},{6,4},{8,10},{10,8},{12,14},{14,12},{16,18},{18,... | collective-permute-start | bytes 3538952 | tf_op jit(solution)/shard_map/ppermute | solution.py:232
  623.3 15.7 %collective-permute-start.31 = (f32[96,1536]{1,0:T(8,128)S(1)}, f32[96,1536]{1,0:T(8,128)S(1)}, u32[]{:S(2)}, u32[]{:S(2)}) collective-permute-start(f32[96,1536]{1,0:T(8,128)S(1)} %get-tuple-element.163), channel_id=1, source_target_pairs={{0,4},{2,6},{4,0},{6,2},{8,12},{10,14},{12,8},{14,10},{16,20},{18,... | collective-permute-start | bytes 1769480 | tf_op jit(solution)/shard_map/ppermute | solution.py:232
  638.5 45.5 %collective-permute-start.5 = (f32[1024,768]{0,1:T(8,128)}, f32[1024,768]{0,1:T(8,128)}, u32[]{:S(2)}, u32[]{:S(2)}) collective-permute-start(f32[1024,768]{0,1:T(8,128)} %add_add_fusion), channel_id=1, source_target_pairs={{0,1},{1,0},{2,3},{3,2},{4,5},{5,4},{6,7},{7,6},{8,9},{9,8},{10,11... | collective-permute-start | bytes 9437192 | tf_op jit(solution)/shard_map/ppermute | solution.py:239
  638.5 29.1 %collective-permute-start.33 = (f32[96,1536]{1,0:T(8,128)S(1)}, f32[96,1536]{1,0:T(8,128)}, u32[]{:S(2)}, u32[]{:S(2)}) collective-permute-start(f32[96,1536]{1,0:T(8,128)S(1)} %get-tuple-element.162), channel_id=1, source_target_pairs={{0,2},{2,0},{4,6},{6,4},{8,10},{10,8},{12,14},{14,12},{16,18},{18,... | collective-permute-start | bytes 1769480 | tf_op jit(solution)/shard_map/ppermute | solution.py:232
  640.2 39.5 %collective-permute-start.32 = (f32[192,1536]{1,0:T(8,128)}, f32[192,1536]{1,0:T(8,128)}, u32[]{:S(2)}, u32[]{:S(2)}) collective-permute-start(f32[192,1536]{1,0:T(8,128)} %maximum_select_fusion.12), channel_id=1, source_target_pairs={{0,2},{2,0},{4,6},{6,4},{8,10},{10,8},{12,14},{14,12},{16,18},{18,... | collective-permute-start | bytes 3538952 | tf_op jit(solution)/shard_map/ppermute | solution.py:232
  647.4 23.0 %collective-permute-start.17 = (f32[2,24,1536]{2,1,0:T(8,128)}, f32[2,24,1536]{2,1,0:T(8,128)}, u32[]{:S(2)}, u32[]{:S(2)}) collective-permute-start(f32[2,24,1536]{2,1,0:T(8,128)} %add_add_fusion.5), channel_id=1, source_target_pairs={{0,16},{2,18},{4,20},{6,22},{8,24},{10,26},{12,28},{14,30},{16,0},... | collective-permute-start | bytes 884744 | tf_op jit(solution)/shard_map/ppermute | solution.py:232
  669.1 29.1 %collective-permute-start.34 = (f32[192,1536]{1,0:T(8,128)S(1)}, f32[192,1536]{1,0:T(8,128)}, u32[]{:S(2)}, u32[]{:S(2)}) collective-permute-start(f32[192,1536]{1,0:T(8,128)S(1)} %maximum_select_fusion.13), channel_id=1, source_target_pairs={{0,4},{2,6},{4,0},{6,2},{8,12},{10,14},{12,8},{14,10},{16,20},{18,... | collective-permute-start | bytes 3538952 | tf_op jit(solution)/shard_map/ppermute | solution.py:232
  671.8 16.9 %collective-permute-start.18 = (f32[2,48,1536]{2,1,0:T(8,128)S(1)}, f32[2,48,1536]{2,1,0:T(8,128)}, u32[]{:S(2)}, u32[]{:S(2)}) collective-permute-start(f32[2,48,1536]{2,1,0:T(8,128)S(1)} %maximum_select_fusion.20), channel_id=1, source_target_pairs={{0,8},{2,10},{4,12},{6,14},{8,0},{10,2},{12,4},{14,6},{16,24},{18,... | collective-permute-start | bytes 1769480 | tf_op jit(solution)/shard_map/ppermute | solution.py:232
  691.0 24.2 %collective-permute-start.19 = (f32[96,1536]{1,0:T(8,128)}, f32[96,1536]{1,0:T(8,128)}, u32[]{:S(2)}, u32[]{:S(2)}) collective-permute-start(f32[96,1536]{1,0:T(8,128)} %get-tuple-element.165), channel_id=1, source_target_pairs={{0,4},{2,6},{4,0},{6,2},{8,12},{10,14},{12,8},{14,10},{16,20},{18,... | collective-permute-start | bytes 1769480 | tf_op jit(solution)/shard_map/ppermute | solution.py:232
  701.5 17.0 %collective-permute-start.21 = (f32[96,1536]{1,0:T(8,128)S(1)}, f32[96,1536]{1,0:T(8,128)}, u32[]{:S(2)}, u32[]{:S(2)}) collective-permute-start(f32[96,1536]{1,0:T(8,128)S(1)} %get-tuple-element.164), channel_id=1, source_target_pairs={{0,2},{2,0},{4,6},{6,4},{8,10},{10,8},{12,14},{14,12},{16,18},{18,... | collective-permute-start | bytes 1769480 | tf_op jit(solution)/shard_map/ppermute | solution.py:232
  714.6 16.9 %collective-permute-start.10 = (f32[8,512]{1,0:T(8,128)S(1)}, f32[8,512]{1,0:T(8,128)S(1)}, u32[]{:S(2)}, u32[]{:S(2)}) collective-permute-start(f32[8,512]{1,0:T(8,128)S(1)} %add.493), channel_id=1, source_target_pairs={{0,16},{2,18},{4,20},{6,22},{8,24},{10,26},{12,28},{14,30},{16,0},... | collective-permute-start | bytes 49160 | tf_op jit(solution)/shard_map/ppermute | solution.py:232
  717.0 25.4 %collective-permute-start.20 = (f32[192,1536]{1,0:T(8,128)S(1)}, f32[192,1536]{1,0:T(8,128)}, u32[]{:S(2)}, u32[]{:S(2)}) collective-permute-start(f32[192,1536]{1,0:T(8,128)S(1)} %maximum_select_fusion.9), channel_id=1, source_target_pairs={{0,2},{2,0},{4,6},{6,4},{8,10},{10,8},{12,14},{14,12},{16,18},{18,... | collective-permute-start | bytes 3538952 | tf_op jit(solution)/shard_map/ppermute | solution.py:232
  720.8 24.9 %collective-permute-start.22 = (f32[192,1536]{1,0:T(8,128)}, f32[192,1536]{1,0:T(8,128)}, u32[]{:S(2)}, u32[]{:S(2)}) collective-permute-start(f32[192,1536]{1,0:T(8,128)} %maximum_select_fusion.10), channel_id=1, source_target_pairs={{0,4},{2,6},{4,0},{6,2},{8,12},{10,14},{12,8},{14,10},{16,20},{18,... | collective-permute-start | bytes 3538952 | tf_op jit(solution)/shard_map/ppermute | solution.py:232
  (137 other events, 1472.7 us)

commit v2 on v0

v2 whole, which is shorter than its diff:
```python
import functools

import jax
import jax.numpy as jnp
from jax import lax
from jax.experimental import pallas as pl
from jax.experimental.pallas import tpu as pltpu
from jax.sharding import PartitionSpec as P

EPSILON = 1e-06
MASKED = -1e30
LANES = 128
NT = (((1,), (1,)), ((), ()))
NN = (((1,), (0,)), ((), ()))


def dot(a, b, dims):
    return lax.dot_general(a, b, dims, preferred_element_type=jnp.float32)


def head_lane_masks(rows, width, half):
    lane = lax.broadcasted_iota(jnp.int32, (rows, 2 * width), 1)
    return (lane < width) if half == 0 else (lane >= width)


def only_head(array, half):
    width = array.shape[1] // 2
    keep = head_lane_masks(array.shape[0], width, half)
    return jnp.where(keep, array.astype(jnp.float32), 0.0).astype(jnp.bfloat16)


def with_mark(array, half, mark):
    rows, both = array.shape
    width = both // 2
    lane = lax.broadcasted_iota(jnp.int32, (rows, both), 1)
    keep = (lane < width) if half == 0 else (lane >= width)
    place = width if half == 0 else 0
    other = jnp.where(lane == place, mark, 0.0)
    return jnp.where(keep, array.astype(jnp.float32), other).astype(jnp.bfloat16)


def key_marks(key_ref, limit):
    rows, both = key_ref.shape
    row = lax.broadcasted_iota(jnp.int32, (rows, both), 0)
    mark = jnp.where(row < limit, 0.0, MASKED)
    keys = key_ref[...]
    return [with_mark(keys, half, mark) for half in range(2)]


def diagonal_bias(line):
    wide = jnp.broadcast_to(line, (LANES, line.shape[1]))
    return pltpu.roll(wide, 0, 1, stride=1, stride_axis=0)


def forward_kernel(causal, block, limit_ref, query_ref, key_ref, value_ref, *rest):
    if causal:
        line_ref, out_ref, log_ref, key_scr, value_scr, bias_scr = rest
    else:
        out_ref, log_ref, key_scr, value_scr = rest
    value_scr[...] = value_ref[...].T
    keys = key_marks(key_ref, limit_ref[0])
    for half in range(2):
        key_scr[half] = keys[half]
        if causal:
            bias_scr[half] = diagonal_bias(line_ref[0, half : half + 1, :])
    rows = query_ref.shape[0]
    key_total = key_ref.shape[0]
    width = query_ref.shape[1] // 2
    for start in range(0, rows, block):
        keys_here = min(key_total, start + block) if causal else key_total
        queries = query_ref[start : start + block, :]
        outs = []
        for half in range(2):
            marked = with_mark(queries, half, 1.0)
            scores = dot(key_scr[half, :keys_here, :], marked, NT)
            if causal:
                parts = []
                for key_at in range(0, keys_here, LANES):
                    lane_at = start - key_at + LANES
                    parts.append(
                        scores[key_at : key_at + LANES]
                        + bias_scr[half, :, lane_at : lane_at + block]
                    )
                scores = jnp.concatenate(parts, axis=0)
            top = jnp.max(scores, axis=0, keepdims=True)
            raised = jnp.exp(scores - top)
            total = jnp.sum(raised, axis=0, keepdims=True)
            mixed = dot(
                value_scr[half * width : (half + 1) * width, :keys_here],
                raised.astype(jnp.bfloat16),
                NN,
            )
            outs.append(mixed / total)
            log_ref[0, half : half + 1, start : start + block] = top + jnp.log(total)
        out_ref[start : start + block, :] = jnp.concatenate(outs, axis=0).T


def smem():
    return pl.BlockSpec(memory_space=pltpu.SMEM)


def attend(queries, keys, values, limit, lines):
    rows, wide = queries.shape
    key_total = keys.shape[0]
    pairs = wide // LANES
    causal = lines is not None
    block = min(256, rows)
    in_specs = [
        smem(),
        pl.BlockSpec((rows, LANES), lambda p: (0, p)),
        pl.BlockSpec((key_total, LANES), lambda p: (0, p)),
        pl.BlockSpec((key_total, LANES), lambda p: (0, p)),
    ]
    scratch = [
        pltpu.VMEM((2, key_total, LANES), jnp.bfloat16),
        pltpu.VMEM((LANES, key_total), jnp.bfloat16),
    ]
    args = [limit, queries, keys, values]
    if causal:
        in_specs.append(pl.BlockSpec((1, 2, lines.shape[2]), lambda p: (p, 0, 0)))
        scratch.append(pltpu.VMEM((2, LANES, lines.shape[2]), jnp.float32))
        args.append(lines)
    return pl.pallas_call(
        functools.partial(forward_kernel, causal, block),
        grid=(pairs,),
        in_specs=in_specs,
        out_specs=[
            pl.BlockSpec((rows, LANES), lambda p: (0, p)),
            pl.BlockSpec((1, 2, rows), lambda p: (p, 0, 0)),
        ],
        out_shape=[
            jax.ShapeDtypeStruct((rows, wide), jnp.float32),
            jax.ShapeDtypeStruct((pairs, 2, rows), jnp.float32),
        ],
        scratch_shapes=scratch,
        compiler_params=pltpu.CompilerParams(vmem_limit_bytes=48 * 1024 * 1024),
        cost_estimate=pl.CostEstimate(
            flops=4 * rows * key_total * wide,
            bytes_accessed=10 * rows * wide,
            transcendentals=rows * key_total * pairs * 2,
        ),
    )(*args)


def backward_kernel(
    causal, block, limit_ref, query_ref, key_ref, value_ref, grad_ref, mixed_ref, log_ref, *rest
):
    if causal:
        line_ref, gq_ref, gk_ref, gv_ref, table_ref, key_scr, key_t_scr, bias_scr, diag_scr, gk_scr, gv_scr = rest
    else:
        gq_ref, gk_ref, gv_ref, key_scr, key_t_scr, gk_scr, gv_scr = rest
    key_t_scr[...] = key_ref[...].T
    keys = key_marks(key_ref, limit_ref[0])
    for half in range(2):
        key_scr[half] = keys[half]
        if causal:
            bias_scr[half] = diagonal_bias(line_ref[0, half : half + 1, :])
            diag_scr[half] = jnp.zeros(diag_scr.shape[1:], jnp.float32)
    gk_scr[...] = jnp.zeros(gk_scr.shape, jnp.float32)
    gv_scr[...] = jnp.zeros(gv_scr.shape, jnp.float32)
    rows = query_ref.shape[0]
    key_total = key_ref.shape[0]
    width = query_ref.shape[1] // 2
    step = 2 * LANES
    for start in range(0, rows, block):
        keys_here = min(key_total, start + block) if causal else key_total
        queries = query_ref[start : start + block, :]
        grads = grad_ref[start : start + block, :]
        inner_t = (grads.astype(jnp.float32) * mixed_ref[start : start + block, :]).T
        query_parts = []
        for half in range(2):
            marked = with_mark(queries, half, 1.0)
            plain = only_head(queries, half)
            grads_here = only_head(grads, half)
            inner = jnp.sum(inner_t[half * width : (half + 1) * width], axis=0, keepdims=True)
            log_total = log_ref[0, half : half + 1, start : start + block]
            grad_queries = jnp.zeros((width, block), jnp.float32)
            for key_at in range(0, keys_here, step):
                here = slice(key_at, key_at + step)
                scores = dot(key_scr[half, here, :], marked, NT)
                if causal:
                    lane_at = start - key_at + LANES
                    bias = jnp.concatenate(
                        [
                            bias_scr[half, :, lane_at : lane_at + block],
                            bias_scr[half, :, lane_at - LANES : lane_at - LANES + block],
                        ],
                        axis=0,
                    )
                    scores = scores + bias
                shares = jnp.exp(scores - log_total)
                grad_shares = dot(value_ref[here, :], grads_here, NT)
                grad_scores = shares * (grad_shares - inner)
                if causal:
                    diag_scr[half, :, lane_at : lane_at + block] += grad_scores[:LANES]
                    diag_scr[half, :, lane_at - LANES : lane_at - LANES + block] += grad_scores[LANES:]
                shares = shares.astype(jnp.bfloat16)
                grad_scores = grad_scores.astype(jnp.bfloat16)
                gv_scr[here, :] += dot(shares, grads_here, NN)
                gk_scr[here, :] += dot(grad_scores, plain, NN)
                grad_queries += dot(key_t_scr[half * width : (half + 1) * width, here], grad_scores, NN)
            query_parts.append(grad_queries)
        gq_ref[start : start + block, :] = (
            jnp.concatenate(query_parts, axis=0).T.astype(jnp.bfloat16)
        )
    gk_ref[...] = gk_scr[...].astype(jnp.bfloat16)
    gv_ref[...] = gv_scr[...].astype(jnp.bfloat16)
    if causal:
        lanes = diag_scr.shape[2]
        down = lax.broadcasted_iota(jnp.int32, (LANES, LANES), 0)
        across = lax.broadcasted_iota(jnp.int32, (LANES, LANES), 1)
        backwards = jnp.where(down + across == LANES - 1, 1.0, 0.0)
        for half in range(2):
            turned = lax.dot_general(
                backwards, diag_scr[half], NN, precision=lax.Precision.HIGHEST
            )
            straight = pltpu.roll(turned, lanes - LANES + 1, 1, stride=1, stride_axis=0)
            table_ref[0, half : half + 1, :] = jnp.sum(straight, axis=0, keepdims=True)


def attend_back(queries, keys, values, grads, mixed, logs, limit, lines):
    rows, wide = queries.shape
    key_total = keys.shape[0]
    pairs = wide // LANES
    causal = lines is not None
    block = min(256, rows)
    tall = pl.BlockSpec((rows, LANES), lambda p: (0, p))
    by_key = pl.BlockSpec((key_total, LANES), lambda p: (0, p))
    in_specs = [
        smem(),
        tall,
        by_key,
        by_key,
        tall,
        tall,
        pl.BlockSpec((1, 2, rows), lambda p: (p, 0, 0)),
    ]
    args = [limit, queries, keys, values, grads, mixed, logs]
    out_specs = [tall, by_key, by_key]
    out_shape = [
        jax.ShapeDtypeStruct((rows, wide), jnp.bfloat16),
        jax.ShapeDtypeStruct((key_total, wide), jnp.bfloat16),
        jax.ShapeDtypeStruct((key_total, wide), jnp.bfloat16),
    ]
    scratch = [
        pltpu.VMEM((2, key_total, LANES), jnp.bfloat16),
        pltpu.VMEM((LANES, key_total), jnp.bfloat16),
    ]
    if causal:
        lanes = lines.shape[2]
        in_specs.append(pl.BlockSpec((1, 2, lanes), lambda p: (p, 0, 0)))
        args.append(lines)
        out_specs.append(pl.BlockSpec((1, 2, lanes), lambda p: (p, 0, 0)))
        out_shape.append(jax.ShapeDtypeStruct((pairs, 2, lanes), jnp.float32))
        scratch += [pltpu.VMEM((2, LANES, lanes), jnp.float32)] * 2
    scratch += [pltpu.VMEM((key_total, LANES), jnp.float32)] * 2
    return pl.pallas_call(
        functools.partial(backward_kernel, causal, block),
        grid=(pairs,),
        in_specs=in_specs,
        out_specs=out_specs,
        out_shape=out_shape,
        scratch_shapes=scratch,
        compiler_params=pltpu.CompilerParams(vmem_limit_bytes=48 * 1024 * 1024),
        cost_estimate=pl.CostEstimate(
            flops=10 * rows * key_total * wide,
            bytes_accessed=20 * rows * wide,
            transcendentals=rows * key_total * pairs * 2,
        ),
    )(*args)


def bias_lines(distance_bucket, position_table):
    buckets, heads = position_table.shape
    total = distance_bucket.shape[0]
    hot = distance_bucket[:, None, None] == jnp.arange(buckets)[None, :, None]
    by_distance = jnp.sum(jnp.where(hot, position_table[None], 0.0), axis=1).T
    edge = jnp.full((heads, LANES), MASKED, jnp.float32)
    lines = jnp.concatenate([edge, by_distance, edge], axis=1)
    return lines.reshape(heads // 2, 2, total + 2 * LANES)


def table_grad(lines, distance_bucket, buckets):
    pairs, two, lanes = lines.shape
    by_distance = lines.reshape(pairs * two, lanes)[:, LANES : lanes - LANES]
    hot = distance_bucket[None, :] == jnp.arange(buckets)[:, None]
    return jnp.sum(jnp.where(hot[:, None, :], by_distance[None], 0.0), axis=-1)


def flip(array, bit):
    size = lax.axis_size("dp")
    return lax.ppermute(array, "dp", [(i, i ^ (1 << bit)) for i in range(size)])


def core_sum(array):
    if lax.axis_size("tensor") != 2:
        return lax.psum(array, "tensor")
    return array + lax.ppermute(array, "tensor", [(0, 1), (1, 0)])


def bit_of(bit):
    return (lax.axis_index("dp") >> bit) & 1


def part_of(array, upper, axis):
    half = array.shape[axis] // 2
    return lax.dynamic_slice_in_dim(array, upper * half, half, axis)


def halve(terms, bit, axis):
    mine = bit_of(bit)
    send = sum(part_of(t, 1 - mine, axis) for t in terms)
    keep = sum(part_of(t, mine, axis) for t in terms)
    return [keep, flip(send, bit)]


def double(array, bit, axis):
    other = flip(array, bit)
    low = jnp.concatenate([array, other], axis=axis)
    high = jnp.concatenate([other, array], axis=axis)
    return jnp.where(bit_of(bit) == 0, low, high)


def pair_sum(first, second, axis):
    if lax.axis_size("dp") != 16:
        return lax.psum((first, second), "dp")
    terms_a = halve([first], 0, axis)
    terms_b = halve([second], 1, axis)
    terms_a = halve(terms_a, 1, axis)
    terms_b = halve(terms_b, 0, axis)
    terms = [jnp.stack([a, b]) for a, b in zip(terms_a, terms_b)]
    terms = halve(terms, 2, axis + 1)
    terms = halve(terms, 3, axis + 1)
    own = terms[0] + terms[1]
    own = double(own, 3, axis + 1)
    own = double(own, 2, axis + 1)
    a = double(own[0], 1, axis)
    b = double(own[1], 0, axis)
    a = double(a, 0, axis)
    b = double(b, 1, axis)
    return a, b


def small_sum(array):
    if lax.axis_size("dp") != 16:
        return lax.psum(array, "dp")
    for bit in range(4):
        array = array + flip(array, bit)
    return array


def matrix_product(former, latter):
    return jnp.dot(former, latter, preferred_element_type=jnp.float32)


def left_contract(former, latter):
    return jnp.einsum("ti,tj->ij", former, latter, preferred_element_type=jnp.float32)


def right_contract(former, latter):
    return jnp.einsum("ti,ji->tj", former, latter, preferred_element_type=jnp.float32)


def normalize(hidden, norm_gain):
    inverse_rms = lax.rsqrt(jnp.mean(hidden * hidden, axis=-1, keepdims=True) + EPSILON)
    return (hidden * inverse_rms * norm_gain, inverse_rms)


def norm_back(hidden, inverse_rms, norm_gain, grad_normed):
    grad_gain = jnp.sum(grad_normed * hidden * inverse_rms, axis=0)
    grad_scaled = grad_normed * norm_gain
    inner_sum = jnp.mean(grad_scaled * hidden, axis=-1, keepdims=True)
    cubed = inverse_rms * inverse_rms * inverse_rms
    return (inverse_rms * grad_scaled - hidden * cubed * inner_sum, grad_gain)


def body(
    decoder_input,
    encoder_output,
    cotangent,
    target_length,
    source_length,
    identifier_tags,
    distance_bucket,
    self_gain,
    self_query,
    self_attention_key,
    self_value,
    self_output,
    position_table,
    cross_gain,
    cross_query,
    cross_key,
    cross_value,
    cross_output,
    hidden_gain,
    hidden_in,
    hidden_out,
):
    item_count, target, model_width = decoder_input.shape
    source = encoder_output.shape[1]
    low = jnp.bfloat16
    decoder_rows = decoder_input.reshape(item_count * target, model_width).astype(jnp.float32)
    encoder_rows = encoder_output.reshape(item_count * source, model_width)
    lines = bias_lines(distance_bucket, position_table)

    normed_one, rms_one = normalize(decoder_rows, self_gain)
    input_one = normed_one.astype(low)
    queries_one = matrix_product(input_one, self_query).astype(low)
    keys_one = matrix_product(input_one, self_attention_key).astype(low)
    values_one = matrix_product(input_one, self_value).astype(low)
    exact_one, logs_one = attend(queries_one, keys_one, values_one, target_length, lines)
    mixed_one = exact_one.astype(low)
    first = decoder_rows + core_sum(matrix_product(mixed_one, self_output))

    second_normalized, rms_two = normalize(first, cross_gain)
    input_two = second_normalized.astype(low)
    queries_two = matrix_product(input_two, cross_query).astype(low)
    keys_two = matrix_product(encoder_rows, cross_key).astype(low)
    values_two = matrix_product(encoder_rows, cross_value).astype(low)
    exact_two, logs_two = attend(queries_two, keys_two, values_two, source_length, None)
    mixed_two = exact_two.astype(low)
    second = first + core_sum(matrix_product(mixed_two, cross_output))

    normed_three, rms_three = normalize(second, hidden_gain)
    input_three = normed_three.astype(low)
    before = matrix_product(input_three, hidden_in)
    gelu_tanh = functools.partial(jax.nn.gelu, approximate=True)
    value, pull = jax.vjp(gelu_tanh, before)
    active = value.astype(low)

    places = jnp.arange(target, dtype=jnp.int32)
    factor = jnp.where(
        places[None, :] < target_length[:, None], 1.0 + identifier_tags.astype(jnp.float32), 0.0
    )
    grad_third = (cotangent.astype(jnp.float32) * factor[:, :, None]).reshape(
        item_count * target, model_width
    )
    grad_branch = grad_third.astype(low)
    hidden = active.shape[1]
    sum_out = pair_sum(
        left_contract(active[:, : hidden // 2], grad_branch),
        left_contract(active[:, hidden // 2 :], grad_branch),
        0,
    )
    grad_active = right_contract(grad_branch, hidden_out)
    grad_before = pull(grad_active)[0].astype(low)
    sum_in = pair_sum(
        left_contract(input_three[:, : model_width // 2], grad_before),
        left_contract(input_three[:, model_width // 2 :], grad_before),
        0,
    )
    third = second + core_sum(matrix_product(active, hidden_out))
    layer_out = third.astype(low).reshape(item_count, target, model_width)

    grad_input_three = core_sum(right_contract(grad_before, hidden_in))
    back_three, grad_hidden_gain = norm_back(second, rms_three, hidden_gain, grad_input_three)
    grad_second = grad_third + back_three
    grad_branch_two = grad_second.astype(low)
    grad_mixed_two = right_contract(grad_branch_two, cross_output).astype(low)
    grad_queries_two, grad_keys_two, grad_values_two = attend_back(
        queries_two,
        keys_two,
        values_two,
        grad_mixed_two,
        exact_two,
        logs_two,
        source_length,
        None,
    )
    grad_input_two = core_sum(right_contract(grad_queries_two, cross_query))
    sum_cross = pair_sum(
        jnp.stack(
            [
                left_contract(input_two, grad_queries_two),
                left_contract(encoder_rows, grad_keys_two),
            ]
        ),
        jnp.stack(
            [
                left_contract(encoder_rows, grad_values_two),
                left_contract(grad_branch_two, mixed_two),
            ]
        ),
        1,
    )
    grad_encoder = core_sum(
        right_contract(grad_keys_two, cross_key) + right_contract(grad_values_two, cross_value)
    )
    back_two, grad_cross_gain = norm_back(first, rms_two, cross_gain, grad_input_two)
    grad_first = grad_second + back_two
    grad_branch_one = grad_first.astype(low)
    grad_mixed_one = right_contract(grad_branch_one, self_output).astype(low)
    grad_queries_one, grad_keys_one, grad_values_one, grad_lines = attend_back(
        queries_one,
        keys_one,
        values_one,
        grad_mixed_one,
        exact_one,
        logs_one,
        target_length,
        lines,
    )
    grad_table = table_grad(grad_lines, distance_bucket, position_table.shape[0])
    grad_input_one = core_sum(
        right_contract(grad_queries_one, self_query)
        + right_contract(grad_keys_one, self_attention_key)
        + right_contract(grad_values_one, self_value)
    )
    sum_self = pair_sum(
        jnp.stack(
            [
                left_contract(input_one, grad_queries_one),
                left_contract(input_one, grad_keys_one),
            ]
        ),
        jnp.stack(
            [
                left_contract(input_one, grad_values_one),
                left_contract(grad_branch_one, mixed_one),
            ]
        ),
        1,
    )
    back_one, grad_self_gain = norm_back(decoder_rows, rms_one, self_gain, grad_input_one)
    grad_decoder = (grad_first + back_one).reshape(item_count, target, model_width)
    grad_encoder = grad_encoder.reshape(item_count, source, model_width)

    flat = jnp.concatenate(
        [grad_self_gain, grad_cross_gain, grad_hidden_gain, grad_table.reshape(-1)]
    )
    lanes = 512
    flat = jnp.pad(flat, (0, -flat.shape[0] % (8 * lanes))).reshape(-1, lanes)
    flat = small_sum(flat).reshape(-1)
    gains = [flat[i * model_width : (i + 1) * model_width] for i in range(3)]
    table = flat[3 * model_width : 3 * model_width + grad_table.size].reshape(grad_table.shape)
    return (
        layer_out,
        grad_decoder,
        grad_encoder,
        gains[0],
        sum_self[0][0],
        sum_self[0][1],
        sum_self[1][0],
        sum_self[1][1].T,
        table,
        gains[1],
        sum_cross[0][0],
        sum_cross[0][1],
        sum_cross[1][0],
        sum_cross[1][1].T,
        gains[2],
        jnp.concatenate(sum_in, axis=0),
        jnp.concatenate(sum_out, axis=0),
    )


def solution(mesh):
    by_item = P("dp", None, None)
    columns = P(None, "tensor")
    rows = P("tensor", None)
    attention = (P(), columns, columns, columns, rows)
    return jax.shard_map(
        body,
        mesh=mesh,
        in_specs=(by_item, by_item, by_item, P("dp"), P("dp"), P("dp", None), P())
        + attention
        + (columns,)
        + attention
        + (P(), columns, rows),
        out_specs=(by_item, by_item, by_item)
        + attention
        + (columns,)
        + attention
        + (P(), columns, rows),
        check_vma=False,
    )
```

time: 953 us -> 594 us (0.62)
  matrix products: 264 us -> 57 us
  waiting for transfers between devices: 473 us -> 277 us
  blocking collectives: 81.4 us -> 0 us
  starting transfers between devices: 1.64 us -> 64.6 us
  Pallas kernels: 0 us -> 56.3 us
  other arithmetic: 66.1 us -> 91.3 us
  between operations: 18.3 us -> 4.14 us
    psum x6 -> x0, waiting for transfers between devices: 473 us -> none  [the longest x1 400 us: body(): lax.psum((grad_self_gain, grad_self_query, grad_self_key, grad_self_value...]
    ppermute x0 -> x59, waiting for transfers between devices: none -> 277 us  [the longest x52 271 us: flip(): return lax.ppermute(array, 'dp', [(i, i ^ 1 << bit) for i in range(size)])]
    dot_general x28 -> x0, matrix products: 183 us -> none  [the longest x2 51.3 us: lookup_bias(): jnp.einsum('ptn,po->otn', one_hot_encoding.astype(jnp.float32), position_...]
    psum x1 -> x0, blocking collectives: 81.4 us -> none  [body(): lax.psum((grad_self_gain, grad_self_query, grad_self_key, grad_self_value...]
    ppermute x0 -> x59, starting transfers between devices: none -> 64.6 us  [the longest x52 63.7 us: flip(): return lax.ppermute(array, 'dp', [(i, i ^ 1 << bit) for i in range(size)])]
    pallas_call x0 -> x4, Pallas kernels: none -> 56.3 us  [the longest x2 32.3 us: attend_back(): pl.pallas_call(functools.partial(backward_kernel, causal, block), grid=(p...]
    select_n x0 -> x24, other arithmetic: none -> 29.4 us  [double(): return jnp.where(bit_of(bit) == 0, low, high)]
    convert_element_type x3 -> x1, other arithmetic: 24 us -> 0.31 us  [body(): input_three = normed_three.astype(low)]
  transfers between devices with their start and end apart: 6 -> 59, of which waited for: 5 -> 30; matrix products, arithmetic and copies ran while one was open for 11% -> 22% of each run, Pallas kernels for 0% -> 6%
where the time goes in v2:
time: 594 us; the launch traced here: 585 us
  waiting for transfers between devices  277 us (47%)
  other arithmetic  91.3 us (15%)
  starting transfers between devices  64.6 us (11%)
  matrix products  57 us (10%)
  Pallas kernels  56.3 us (9%)
  local copies, waits for them, and re-layouts  33.9 us (6%)
    ppermute x52, waiting for transfers between devices, flip(): return lax.ppermute(array, 'dp', [(i, i ^ 1 << bit) for i in range(size)])  271 us
    ppermute x52, starting transfers between devices, flip(): return lax.ppermute(array, 'dp', [(i, i ^ 1 << bit) for i in range(size)])  63.7 us
    pallas_call x2, Pallas kernels, attend_back(): pl.pallas_call(functools.partial(backward_kernel, causal, block), grid=(p...  32.3 us
    select_n x24, other arithmetic, double(): return jnp.where(bit_of(bit) == 0, low, high)  29.4 us
    unnamed x134, local copies, waits for them, and re-layouts  25.1 us
    pallas_call x2, Pallas kernels, attend(): pl.pallas_call(functools.partial(forward_kernel, causal, block), grid=(pa...  24 us
    dot_general x10, matrix products, right_contract(): jnp.einsum('ti,ji->tj', former, latter, preferred_element_type=jnp.float32)  22.6 us
    dot_general x10, matrix products, matrix_product(): return jnp.dot(former, latter, preferred_element_type=jnp.float32)  21.4 us
  transfers between devices with their start and end apart: 59, of which 30 were waited for; matrix products, arithmetic and copies ran while one was open for 22% of the time, Pallas kernels for 6%

profile of v2, /device:TPU:0, one launch (start us, length us, event | category | flops | bytes accessed | tf_op | source)
XLA Modules:
  0.0 584.7 jit_solution(3906308505204518325)
XLA Ops:
  16.0 12.7 %shard_map.332 = (f32[1024,384]{1,0:T(8,128)S(1)}, f32[3,2,1024]{2,1,0:T(2,128)S(1)}) custom-call(s32[1]{0:T(128)} %copy.103.limit_ref, bf16[1024,384]{1,0:T(8,128)(2,1)S(1)} %convolution_convert_fusion.5.query_ref, bf16[1024,384]{1,0:T(8,128)(2,1)S(1)} %copy-done.10, bf16[1024,384]{1,0:T(8,128)(2,1)S(1)} %copy-done.12, f32[3,2,1280]{2,1,0:T(2,128)S(1)} %reshape.185.rest_0_), custom_call_target="tpu_custom_call" | custom-call | flops 1610612736 | bytes 3932160 | tf_op jit(solution)/shard_map/pallas_call | solution.py:123
  32.2 3.4 collective-permute-done
  38.0 11.3 %shard_map.333 = (f32[1024,384]{1,0:T(8,128)S(1)}, f32[3,2,1024]{2,1,0:T(2,128)S(1)}) custom-call(s32[1]{0:T(128)S(6)} %copy.104.limit_ref, bf16[1024,384]{1,0:T(8,128)(2,1)S(1)} %convolution_convert_fusion.2.query_ref, bf16[512,384]{1,0:T(8,128)(2,1)S(1)} %convolution_convert_fusion.7.key_ref, bf16[512,384]{1,0:T(8,128)(2,1)S(1)} %convolution_convert_fusion.6.value_ref), custom_call_target="tpu_custom_call" | custom-call | flops 805306368 | bytes 3932160 | tf_op jit(solution)/shard_map/pallas_call | solution.py:123
  55.0 3.0 collective-permute-done.1
  58.0 5.0 multiply_reduce_fusion.4
  64.7 4.1 multiply_convert_fusion
  68.8 6.5 %fusion.6 = bf16[1024,1536]{1,0:T(8,128)(2,1)S(1)} fusion(f32[1024,1536]{1,0:T(8,128)S(1)} %get-tuple-element.152, bf16[1536,768]{1,0:T(8,128)(2,1)S(1)} %copy-done.62, bf16[1,1024,768]{1,2,0:T(8,128)(2,1)S(1)} %copy-done.27, f32[1024]{0:T(1024)S(1)} %bitcast.171), kind=kOutput, calls=%fused_computation.14 | convolution fusion | flops 2449735680 | bytes 13373440 | tf_op jit(solution)/shard_map/ti,ji->tj/dot_general | solution.py:361
  78.2 2.9 collective-permute-start.35
  86.5 4.3 fusion.97
  90.8 17.1 %collective-permute-done.35 = f32[192,1536]{1,0:T(8,128)S(1)} collective-permute-done((f32[192,1536]{1,0:T(8,128)S(1)}, f32[192,1536]{1,0:T(8,128)S(1)}, u32[]{:S(2)}, u32[]{:S(2)}) %collective-permute-start.35) | collective-permute-done | bytes 1179680 | tf_op jit(solution)/shard_map/ppermute | solution.py:292
  112.0 21.1 %collective-permute-done.47 = f32[384,768]{1,0:T(8,128)S(1)} collective-permute-done((f32[384,768]{1,0:T(8,128)S(1)}, f32[384,768]{1,0:T(8,128)S(1)}, u32[]{:S(2)}, u32[]{:S(2)}) %collective-permute-start.47) | collective-permute-done | bytes 1179680 | tf_op jit(solution)/shard_map/ppermute | solution.py:292
  138.7 4.4 fusion.96
  143.0 5.0 collective-permute-done.37
  150.6 9.1 %collective-permute-done.49 = f32[192,768]{1,0:T(8,128)} collective-permute-done((f32[192,768]{1,0:T(8,128)}, f32[192,768]{1,0:T(8,128)}, u32[]{:S(2)}, u32[]{:S(2)}) %collective-permute-start.49) | collective-permute-done | bytes 589856 | tf_op jit(solution)/shard_map/ppermute | solution.py:292
  169.1 14.8 %collective-permute-done.51 = f32[2,96,768]{2,1,0:T(8,128)S(1)} collective-permute-done((f32[2,96,768]{2,1,0:T(8,128)}, f32[2,96,768]{2,1,0:T(8,128)S(1)}, u32[]{:S(2)}, u32[]{:S(2)}) %collective-permute-start.51) | collective-permute-done | bytes 589856 | tf_op jit(solution)/shard_map/ppermute | solution.py:292
  188.0 19.1 %collective-permute-done.52 = f32[2,48,768]{2,1,0:T(8,128)} collective-permute-done((f32[2,48,768]{2,1,0:T(8,128)S(1)}, f32[2,48,768]{2,1,0:T(8,128)}, u32[]{:S(2)}, u32[]{:S(2)}) %collective-permute-start.52) | collective-permute-done | bytes 294944 | tf_op jit(solution)/shard_map/ppermute | solution.py:292
  208.2 11.4 %collective-permute-done.41 = f32[2,24,1536]{2,1,0:T(8,128)S(1)} collective-permute-done((f32[2,24,1536]{2,1,0:T(8,128)S(1)}, f32[2,24,1536]{2,1,0:T(8,128)S(1)}, u32[]{:S(2)}, u32[]{:S(2)}) %collective-permute-start.41) | collective-permute-done | bytes 294944 | tf_op jit(solution)/shard_map/ppermute | solution.py:292
  219.8 5.2 collective-permute-done.53
  225.1 5.3 multiply_reduce_fusion
  230.5 6.6 %bitcast_add_fusion = (f32[1024,768]{0,1:T(8,128)S(1)}, bf16[1,1024,768]{1,2,0:T(8,128)(2,1)}) fusion(f32[1024,768]{0,1:T(8,128)S(1)} %copy-done.20, bf16[1,1024,768]{1,2,0:T(8,128)(2,1)S(1)} %copy-done.28, f32[1024]{0:T(1024)S(1)} %broadcast_multiply_fusion.2, f32[1024]{0:T(1024)S(1)} %copy-done.57, f32[1024]{0:T(1024)S(1)} %bitcast.174, ...), kind=kLoop, calls=%fused_computation.52 | loop fusion | flops 9437184 | bytes 22039552 | tf_op jit(solution)/shard_map/add | solution.py:458
  240.8 12.7 %shard_map.334 = (bf16[1024,384]{1,0:T(8,128)(2,1)S(1)}, bf16[512,384]{1,0:T(8,128)(2,1)S(1)}, bf16[512,384]{1,0:T(8,128)(2,1)S(1)}) custom-call(s32[1]{0:T(128)S(6)} %copy.104.limit_ref, bf16[1024,384]{1,0:T(8,128)(2,1)S(1)} %copy-done.7, bf16[512,384]{1,0:T(8,128)(2,1)S(1)} %convolution_convert_fusion.7.key_ref, ...), custom_call_target="tpu_custom_call" | custom-call | flops 2013265920 | bytes 7864320 | tf_op jit(solution)/shard_map/pallas_call | solution.py:257
  264.0 19.0 %collective-permute-done.23 = f32[2,384,384]{2,1,0:T(8,128)S(1)} collective-permute-done((f32[2,384,384]{2,1,0:T(8,128)S(1)}, f32[2,384,384]{2,1,0:T(8,128)S(1)}, u32[]{:S(2)}, u32[]{:S(2)}) %collective-permute-start.23) | collective-permute-done | bytes 1179680 | tf_op jit(solution)/shard_map/ppermute | solution.py:292
  288.7 9.3 %collective-permute-done.25 = f32[2,192,384]{2,1,0:T(8,128)S(1)} collective-permute-done((f32[2,192,384]{2,1,0:T(8,128)S(1)}, f32[2,192,384]{2,1,0:T(8,128)S(1)}, u32[]{:S(2)}, u32[]{:S(2)}) %collective-permute-start.25) | collective-permute-done | bytes 589856 | tf_op jit(solution)/shard_map/ppermute | solution.py:292
  307.4 8.0 %collective-permute-done.45 = f32[96,1536]{1,0:T(8,128)} collective-permute-done((f32[96,1536]{1,0:T(8,128)S(1)}, f32[96,1536]{1,0:T(8,128)}, u32[]{:S(2)}, u32[]{:S(2)}) %collective-permute-start.45) | collective-permute-done | bytes 589856 | tf_op jit(solution)/shard_map/ppermute | solution.py:292
  318.7 6.9 %collective-permute-done.57 = f32[192,768]{1,0:T(8,128)} collective-permute-done((f32[192,768]{1,0:T(8,128)}, f32[192,768]{1,0:T(8,128)}, u32[]{:S(2)}, u32[]{:S(2)}) %collective-permute-start.57) | collective-permute-done | bytes 589856 | tf_op jit(solution)/shard_map/ppermute | solution.py:292
  331.6 3.1 collective-permute-start.28
  334.7 3.2 add_bitcast_fusion
  337.9 7.0 %collective-permute-done.28 = f32[2,2,48,384]{3,2,1,0:T(8,128)S(1)} collective-permute-done((f32[2,2,48,384]{3,2,1,0:T(8,128)S(1)}, f32[2,2,48,384]{3,2,1,0:T(8,128)S(1)}, u32[]{:S(2)}, u32[]{:S(2)}) %collective-permute-start.28) | collective-permute-done | bytes 294944 | tf_op jit(solution)/shard_map/ppermute | solution.py:292
  345.1 9.5 %collective-permute-done.46 = f32[192,1536]{1,0:T(8,128)S(1)} collective-permute-done((f32[192,1536]{1,0:T(8,128)S(1)}, f32[192,1536]{1,0:T(8,128)S(1)}, u32[]{:S(2)}, u32[]{:S(2)}) %collective-permute-start.46) | collective-permute-done | bytes 1179680 | tf_op jit(solution)/shard_map/ppermute | solution.py:292
  354.8 5.7 collective-permute-done.29
  360.6 4.1 multiply_reduce_fusion.1
  364.7 3.9 subtract_add_fusion
  372.8 19.6 %shard_map.335 = (bf16[1024,384]{1,0:T(8,128)(2,1)S(1)}, bf16[1024,384]{1,0:T(8,128)(2,1)S(1)}, bf16[1024,384]{1,0:T(8,128)(2,1)S(1)}, f32[3,2,1280]{2,1,0:T(2,128)S(1)}) custom-call(s32[1]{0:T(128)} %copy.103.limit_ref, bf16[1024,384]{1,0:T(8,128)(2,1)S(1)} %copy-done.9, bf16[1024,384]{1,0:T(8,128)(2,1)S(1)} %copy-done.11, ...), custom_call_target="tpu_custom_call" | custom-call | flops 4026531840 | bytes 7864320 | tf_op jit(solution)/shard_map/pallas_call | solution.py:257
  403.0 18.9 %collective-permute-done.11 = f32[2,384,384]{2,1,0:T(8,128)S(1)} collective-permute-done((f32[2,384,384]{2,1,0:T(8,128)S(1)}, f32[2,384,384]{2,1,0:T(8,128)S(1)}, u32[]{:S(2)}, u32[]{:S(2)}) %collective-permute-start.11) | collective-permute-done | bytes 1179680 | tf_op jit(solution)/shard_map/ppermute | solution.py:292
  429.5 8.4 %collective-permute-done.13 = f32[2,192,384]{2,1,0:T(8,128)S(1)} collective-permute-done((f32[2,192,384]{2,1,0:T(8,128)S(1)}, f32[2,192,384]{2,1,0:T(8,128)S(1)}, u32[]{:S(2)}, u32[]{:S(2)}) %collective-permute-start.13) | collective-permute-done | bytes 589856 | tf_op jit(solution)/shard_map/ppermute | solution.py:292
  447.7 2.9 collective-permute-done.31
  454.1 12.5 %collective-permute-done.56 = f32[384,768]{1,0:T(8,128)S(1)} collective-permute-done((f32[384,768]{1,0:T(8,128)S(1)}, f32[384,768]{1,0:T(8,128)S(1)}, u32[]{:S(2)}, u32[]{:S(2)}) %collective-permute-start.56) | collective-permute-done | bytes 1179680 | tf_op jit(solution)/shard_map/ppermute | solution.py:292
  472.8 11.3 %collective-permute-done.16 = f32[2,2,48,384]{3,2,1,0:T(8,128)} collective-permute-done((f32[2,2,48,384]{3,2,1,0:T(8,128)S(1)}, f32[2,2,48,384]{3,2,1,0:T(8,128)}, u32[]{:S(2)}, u32[]{:S(2)}) %collective-permute-start.16) | collective-permute-done | bytes 294944 | tf_op jit(solution)/shard_map/ppermute | solution.py:292
  485.3 16.9 %collective-permute-done.33 = f32[2,192,384]{2,1,0:T(8,128)} collective-permute-done((f32[2,192,384]{2,1,0:T(8,128)S(1)}, f32[2,192,384]{2,1,0:T(8,128)}, u32[]{:S(2)}, u32[]{:S(2)}) %collective-permute-start.33) | collective-permute-done | bytes 589856 | tf_op jit(solution)/shard_map/ppermute | solution.py:292
  505.6 3.0 maximum_select_fusion.2
  511.9 4.1 fusion.16
  515.9 4.9 collective-permute-done.18
  523.9 9.9 %collective-permute-done.34 = f32[2,384,384]{2,1,0:T(8,128)} collective-permute-done((f32[2,384,384]{2,1,0:T(8,128)}, f32[2,384,384]{2,1,0:T(8,128)}, u32[]{:S(2)}, u32[]{:S(2)}) %collective-permute-start.34) | collective-permute-done | bytes 1179680 | tf_op jit(solution)/shard_map/ppermute | solution.py:292
  533.8 2.8 maximum_select_fusion.3
  554.0 5.4 fusion.13
  559.5 3.5 copy.90
  564.4 8.5 %collective-permute-done.20 = f32[2,384,384]{2,1,0:T(8,128)} collective-permute-done((f32[2,384,384]{2,1,0:T(8,128)}, f32[2,384,384]{2,1,0:T(8,128)}, u32[]{:S(2)}, u32[]{:S(2)}) %collective-permute-start.20) | collective-permute-done | bytes 1179680 | tf_op jit(solution)/shard_map/ppermute | solution.py:292
  573.0 2.8 maximum_select_fusion
  (340 shorter events, 180.6 us)
Async XLA Ops:
  78.2 29.6 %collective-permute-start.35 = (f32[192,1536]{1,0:T(8,128)S(1)}, f32[192,1536]{1,0:T(8,128)S(1)}, u32[]{:S(2)}, u32[]{:S(2)}) collective-permute-start(f32[192,1536]{1,0:T(8,128)S(1)} %constant_dynamic-slice_fusion.2), channel_id=1, source_target_pairs={{0,2},{2,0},{4,6},{6,4},{8,10},{10,8},{12,14},{14,12},{16,18},{18,... | collective-permute-start | bytes 3538952 | tf_op jit(solution)/shard_map/ppermute | solution.py:292
  81.2 29.1 %collective-permute-start.36 = (f32[192,1536]{1,0:T(8,128)S(1)}, f32[192,1536]{1,0:T(8,128)S(1)}, u32[]{:S(2)}, u32[]{:S(2)}) collective-permute-start(f32[192,1536]{1,0:T(8,128)S(1)} %constant_dynamic-slice_fusion.1), channel_id=1, source_target_pairs={{0,4},{2,6},{4,0},{6,2},{8,12},{10,14},{12,8},{14,10},{16,20},{18,... | collective-permute-start | bytes 3538952 | tf_op jit(solution)/shard_map/ppermute | solution.py:292
  85.7 47.4 %collective-permute-start.47 = (f32[384,768]{1,0:T(8,128)S(1)}, f32[384,768]{1,0:T(8,128)S(1)}, u32[]{:S(2)}, u32[]{:S(2)}) collective-permute-start(f32[384,768]{1,0:T(8,128)S(1)} %constant_dynamic-slice_fusion.3), channel_id=1, source_target_pairs={{0,2},{2,0},{4,6},{6,4},{8,10},{10,8},{12,14},{14,12},{16,18},{18,... | collective-permute-start | bytes 3538952 | tf_op jit(solution)/shard_map/ppermute | solution.py:292
  86.4 49.8 %collective-permute-start.48 = (f32[384,768]{1,0:T(8,128)S(1)}, f32[384,768]{1,0:T(8,128)S(1)}, u32[]{:S(2)}, u32[]{:S(2)}) collective-permute-start(f32[384,768]{1,0:T(8,128)S(1)} %constant_dynamic-slice_fusion), channel_id=1, source_target_pairs={{0,4},{2,6},{4,0},{6,2},{8,12},{10,14},{12,8},{14,10},{16,20},{18,... | collective-permute-start | bytes 3538952 | tf_op jit(solution)/shard_map/ppermute | solution.py:292
  90.8 134.3 %collective-permute-start.3 = (f32[1024,768]{0,1:T(8,128)}, f32[1024,768]{0,1:T(8,128)}, u32[]{:S(2)}, u32[]{:S(2)}) collective-permute-start(f32[1024,768]{0,1:T(8,128)} %fusion.97), channel_id=1, source_target_pairs={{0,1},{1,0},{2,3},{3,2},{4,5},{5,4},{6,7},{7,6},{8,9},{9,8},{10,11... | collective-permute-start | bytes 9437192 | tf_op jit(solution)/shard_map/ppermute | solution.py:298
  108.1 39.9 %collective-permute-start.37 = (f32[96,1536]{1,0:T(8,128)S(1)}, f32[96,1536]{1,0:T(8,128)S(1)}, u32[]{:S(2)}, u32[]{:S(2)}) collective-permute-start(f32[96,1536]{1,0:T(8,128)S(1)} %get-tuple-element.107), channel_id=1, source_target_pairs={{0,4},{2,6},{4,0},{6,2},{8,12},{10,14},{12,8},{14,10},{16,20},{18,... | collective-permute-start | bytes 1769480 | tf_op jit(solution)/shard_map/ppermute | solution.py:292
  110.5 37.5 %collective-permute-start.38 = (f32[96,1536]{1,0:T(8,128)S(1)}, f32[96,1536]{1,0:T(8,128)S(1)}, u32[]{:S(2)}, u32[]{:S(2)}) collective-permute-start(f32[96,1536]{1,0:T(8,128)S(1)} %get-tuple-element.105), channel_id=1, source_target_pairs={{0,2},{2,0},{4,6},{6,4},{8,10},{10,8},{12,14},{14,12},{16,18},{18,... | collective-permute-start | bytes 1769480 | tf_op jit(solution)/shard_map/ppermute | solution.py:292
  134.1 25.5 %collective-permute-start.49 = (f32[192,768]{1,0:T(8,128)}, f32[192,768]{1,0:T(8,128)}, u32[]{:S(2)}, u32[]{:S(2)}) collective-permute-start(f32[192,768]{1,0:T(8,128)} %get-tuple-element.103), channel_id=1, source_target_pairs={{0,4},{2,6},{4,0},{6,2},{8,12},{10,14},{12,8},{14,10},{16,20},{18,... | collective-permute-start | bytes 1769480 | tf_op jit(solution)/shard_map/ppermute | solution.py:292
  137.2 22.5 %collective-permute-start.50 = (f32[192,768]{1,0:T(8,128)}, f32[192,768]{1,0:T(8,128)}, u32[]{:S(2)}, u32[]{:S(2)}) collective-permute-start(f32[192,768]{1,0:T(8,128)} %get-tuple-element.101), channel_id=1, source_target_pairs={{0,2},{2,0},{4,6},{6,4},{8,10},{10,8},{12,14},{14,12},{16,18},{18,... | collective-permute-start | bytes 1769480 | tf_op jit(solution)/shard_map/ppermute | solution.py:292
  148.0 82.4 %collective-permute-start.2 = (f32[1024,768]{0,1:T(8,128)}, f32[1024,768]{0,1:T(8,128)}, u32[]{:S(2)}, u32[]{:S(2)}) collective-permute-start(f32[1024,768]{0,1:T(8,128)} %fusion.96), channel_id=1, source_target_pairs={{0,1},{1,0},{2,3},{3,2},{4,5},{5,4},{6,7},{7,6},{8,9},{9,8},{10,11... | collective-permute-start | bytes 9437192 | tf_op jit(solution)/shard_map/ppermute | solution.py:298
  149.0 16.4 %collective-permute-start.39 = (f32[2,48,1536]{2,1,0:T(8,128)}, f32[2,48,1536]{2,1,0:T(8,128)}, u32[]{:S(2)}, u32[]{:S(2)}) collective-permute-start(f32[2,48,1536]{2,1,0:T(8,128)} %get-tuple-element.121), channel_id=1, source_target_pairs={{0,8},{2,10},{4,12},{6,14},{8,0},{10,2},{12,4},{14,6},{16,24},{18,... | collective-permute-start | bytes 1769480 | tf_op jit(solution)/shard_map/ppermute | solution.py:292
  161.8 22.1 %collective-permute-start.51 = (f32[2,96,768]{2,1,0:T(8,128)}, f32[2,96,768]{2,1,0:T(8,128)S(1)}, u32[]{:S(2)}, u32[]{:S(2)}) collective-permute-start(f32[2,96,768]{2,1,0:T(8,128)} %get-tuple-element.119), channel_id=1, source_target_pairs={{0,8},{2,10},{4,12},{6,14},{8,0},{10,2},{12,4},{14,6},{16,24},{18,... | collective-permute-start | bytes 1769480 | tf_op jit(solution)/shard_map/ppermute | solution.py:292
  166.4 19.4 %collective-permute-start.40 = (f32[2,24,1536]{2,1,0:T(8,128)S(1)}, f32[2,24,1536]{2,1,0:T(8,128)S(1)}, u32[]{:S(2)}, u32[]{:S(2)}) collective-permute-start(f32[2,24,1536]{2,1,0:T(8,128)S(1)} %dynamic-slice_add_fusion.5), channel_id=1, source_target_pairs={{0,16},{2,18},{4,20},{6,22},{8,24},{10,26},{12,28},{14,30},{16,0},... | collective-permute-start | bytes 884744 | tf_op jit(solution)/shard_map/ppermute | solution.py:292
  183.9 23.1 %collective-permute-start.52 = (f32[2,48,768]{2,1,0:T(8,128)S(1)}, f32[2,48,768]{2,1,0:T(8,128)}, u32[]{:S(2)}, u32[]{:S(2)}) collective-permute-start(f32[2,48,768]{2,1,0:T(8,128)S(1)} %dynamic-slice_add_fusion.4), channel_id=1, source_target_pairs={{0,16},{2,18},{4,20},{6,22},{8,24},{10,26},{12,28},{14,30},{16,0},... | collective-permute-start | bytes 884744 | tf_op jit(solution)/shard_map/ppermute | solution.py:292
  186.8 32.8 %collective-permute-start.41 = (f32[2,24,1536]{2,1,0:T(8,128)S(1)}, f32[2,24,1536]{2,1,0:T(8,128)S(1)}, u32[]{:S(2)}, u32[]{:S(2)}) collective-permute-start(f32[2,24,1536]{2,1,0:T(8,128)S(1)} %add_add_fusion.3), channel_id=1, source_target_pairs={{0,16},{2,18},{4,20},{6,22},{8,24},{10,26},{12,28},{14,30},{16,0},... | collective-permute-start | bytes 884744 | tf_op jit(solution)/shard_map/ppermute | solution.py:292
  208.1 16.8 %collective-permute-start.53 = (f32[2,48,768]{2,1,0:T(8,128)S(1)}, f32[2,48,768]{2,1,0:T(8,128)S(1)}, u32[]{:S(2)}, u32[]{:S(2)}) collective-permute-start(f32[2,48,768]{2,1,0:T(8,128)S(1)} %add_add_fusion.2), channel_id=1, source_target_pairs={{0,16},{2,18},{4,20},{6,22},{8,24},{10,26},{12,28},{14,30},{16,0},... | collective-permute-start | bytes 884744 | tf_op jit(solution)/shard_map/ppermute | solution.py:292
  219.7 44.1 %collective-permute-start.42 = (f32[2,48,1536]{2,1,0:T(8,128)S(1)}, f32[2,48,1536]{2,1,0:T(8,128)S(1)}, u32[]{:S(2)}, u32[]{:S(2)}) collective-permute-start(f32[2,48,1536]{2,1,0:T(8,128)S(1)} %maximum_select_fusion.22), channel_id=1, source_target_pairs={{0,8},{2,10},{4,12},{6,14},{8,0},{10,2},{12,4},{14,6},{16,24},{18,... | collective-permute-start | bytes 1769480 | tf_op jit(solution)/shard_map/ppermute | solution.py:292
  225.0 62.0 %collective-permute-start.54 = (f32[2,96,768]{2,1,0:T(8,128)S(1)}, f32[2,96,768]{2,1,0:T(8,128)S(1)}, u32[]{:S(2)}, u32[]{:S(2)}) collective-permute-start(f32[2,96,768]{2,1,0:T(8,128)S(1)} %maximum_select_fusion.23), channel_id=1, source_target_pairs={{0,8},{2,10},{4,12},{6,14},{8,0},{10,2},{12,4},{14,6},{16,24},{18,... | collective-permute-start | bytes 1769480 | tf_op jit(solution)/shard_map/ppermute | solution.py:292
  255.3 27.7 %collective-permute-start.23 = (f32[2,384,384]{2,1,0:T(8,128)S(1)}, f32[2,384,384]{2,1,0:T(8,128)S(1)}, u32[]{:S(2)}, u32[]{:S(2)}) collective-permute-start(f32[2,384,384]{2,1,0:T(8,128)S(1)} %fusion.24), channel_id=1, source_target_pairs={{0,2},{2,0},{4,6},{6,4},{8,10},{10,8},{12,14},{14,12},{16,18},{18,... | collective-permute-start | bytes 3538952 | tf_op jit(solution)/shard_map/ppermute | solution.py:292
  256.6 28.9 %collective-permute-start.24 = (f32[2,384,384]{2,1,0:T(8,128)S(1)}, f32[2,384,384]{2,1,0:T(8,128)S(1)}, u32[]{:S(2)}, u32[]{:S(2)}) collective-permute-start(f32[2,384,384]{2,1,0:T(8,128)S(1)} %fusion.23), channel_id=1, source_target_pairs={{0,4},{2,6},{4,0},{6,2},{8,12},{10,14},{12,8},{14,10},{16,20},{18,... | collective-permute-start | bytes 3538952 | tf_op jit(solution)/shard_map/ppermute | solution.py:292
  260.9 99.6 %collective-permute-start.4 = (f32[1024,768]{0,1:T(8,128)}, f32[1024,768]{0,1:T(8,128)}, u32[]{:S(2)}, u32[]{:S(2)}) collective-permute-start(f32[1024,768]{0,1:T(8,128)} %fusion.98), channel_id=1, source_target_pairs={{0,1},{1,0},{2,3},{3,2},{4,5},{5,4},{6,7},{7,6},{8,9},{9,8},{10,11... | collective-permute-start | bytes 9437192 | tf_op jit(solution)/shard_map/ppermute | solution.py:298
  263.8 67.8 %collective-permute-start.6 = (f32[512,768]{1,0:T(8,128)}, f32[512,768]{1,0:T(8,128)}, u32[]{:S(2)}, u32[]{:S(2)}) collective-permute-start(f32[512,768]{1,0:T(8,128)} %convolution_add_fusion), channel_id=1, source_target_pairs={{0,1},{1,0},{2,3},{3,2},{4,5},{5,4},{6,7},{7,6},{8,9},{9,8},{10,11... | collective-permute-start | bytes 4718600 | tf_op jit(solution)/shard_map/ppermute | solution.py:298
  284.0 14.1 %collective-permute-start.25 = (f32[2,192,384]{2,1,0:T(8,128)S(1)}, f32[2,192,384]{2,1,0:T(8,128)S(1)}, u32[]{:S(2)}, u32[]{:S(2)}) collective-permute-start(f32[2,192,384]{2,1,0:T(8,128)S(1)} %get-tuple-element.111), channel_id=1, source_target_pairs={{0,4},{2,6},{4,0},{6,2},{8,12},{10,14},{12,8},{14,10},{16,20},{18,... | collective-permute-start | bytes 1769480 | tf_op jit(solution)/shard_map/ppermute | solution.py:292
  286.5 16.3 %collective-permute-start.26 = (f32[2,192,384]{2,1,0:T(8,128)S(1)}, f32[2,192,384]{2,1,0:T(8,128)S(1)}, u32[]{:S(2)}, u32[]{:S(2)}) collective-permute-start(f32[2,192,384]{2,1,0:T(8,128)S(1)} %get-tuple-element.109), channel_id=1, source_target_pairs={{0,2},{2,0},{4,6},{6,4},{8,10},{10,8},{12,14},{14,12},{16,18},{18,... | collective-permute-start | bytes 1769480 | tf_op jit(solution)/shard_map/ppermute | solution.py:292
  287.1 28.4 %collective-permute-start.45 = (f32[96,1536]{1,0:T(8,128)S(1)}, f32[96,1536]{1,0:T(8,128)}, u32[]{:S(2)}, u32[]{:S(2)}) collective-permute-start(f32[96,1536]{1,0:T(8,128)S(1)} %get-tuple-element.137), channel_id=1, source_target_pairs={{0,2},{2,0},{4,6},{6,4},{8,10},{10,8},{12,14},{14,12},{16,18},{18,... | collective-permute-start | bytes 1769480 | tf_op jit(solution)/shard_map/ppermute | solution.py:292
  298.0 17.9 %collective-permute-start.43 = (f32[96,1536]{1,0:T(8,128)S(1)}, f32[96,1536]{1,0:T(8,128)}, u32[]{:S(2)}, u32[]{:S(2)}) collective-permute-start(f32[96,1536]{1,0:T(8,128)S(1)} %get-tuple-element.136), channel_id=1, source_target_pairs={{0,4},{2,6},{4,0},{6,2},{8,12},{10,14},{12,8},{14,10},{16,20},{18,... | collective-permute-start | bytes 1769480 | tf_op jit(solution)/shard_map/ppermute | solution.py:292
  303.5 22.1 %collective-permute-start.57 = (f32[192,768]{1,0:T(8,128)}, f32[192,768]{1,0:T(8,128)}, u32[]{:S(2)}, u32[]{:S(2)}) collective-permute-start(f32[192,768]{1,0:T(8,128)} %get-tuple-element.135), channel_id=1, source_target_pairs={{0,2},{2,0},{4,6},{6,4},{8,10},{10,8},{12,14},{14,12},{16,18},{18,... | collective-permute-start | bytes 1769480 | tf_op jit(solution)/shard_map/ppermute | solution.py:292
  316.0 14.6 %collective-permute-start.27 = (f32[2,2,96,384]{3,2,1,0:T(8,128)S(1)}, f32[2,2,96,384]{3,2,1,0:T(8,128)S(1)}, u32[]{:S(2)}, u32[]{:S(2)}) collective-permute-start(f32[2,2,96,384]{3,2,1,0:T(8,128)S(1)} %get-tuple-element.127), channel_id=1, source_target_pairs={{0,8},{2,10},{4,12},{6,14},{8,0},{10,2},{12,4},{14,6},{16,24},{18,... | collective-permute-start | bytes 1769480 | tf_op jit(solution)/shard_map/ppermute | solution.py:292
  325.6 28.9 %collective-permute-start.46 = (f32[192,1536]{1,0:T(8,128)S(1)}, f32[192,1536]{1,0:T(8,128)S(1)}, u32[]{:S(2)}, u32[]{:S(2)}) collective-permute-start(f32[192,1536]{1,0:T(8,128)S(1)} %maximum_select_fusion.16), channel_id=1, source_target_pairs={{0,4},{2,6},{4,0},{6,2},{8,12},{10,14},{12,8},{14,10},{16,20},{18,... | collective-permute-start | bytes 3538952 | tf_op jit(solution)/shard_map/ppermute | solution.py:292
  329.3 95.7 %collective-permute-start.44 = (f32[192,1536]{1,0:T(8,128)S(1)}, f32[192,1536]{1,0:T(8,128)}, u32[]{:S(2)}, u32[]{:S(2)}) collective-permute-start(f32[192,1536]{1,0:T(8,128)S(1)} %maximum_select_fusion.15), channel_id=1, source_target_pairs={{0,2},{2,0},{4,6},{6,4},{8,10},{10,8},{12,14},{14,12},{16,18},{18,... | collective-permute-start | bytes 3538952 | tf_op jit(solution)/shard_map/ppermute | solution.py:292
  330.5 115.1 %collective-permute-start.58 = (f32[384,768]{1,0:T(8,128)S(1)}, f32[384,768]{1,0:T(8,128)}, u32[]{:S(2)}, u32[]{:S(2)}) collective-permute-start(f32[384,768]{1,0:T(8,128)S(1)} %maximum_select_fusion.19), channel_id=1, source_target_pairs={{0,4},{2,6},{4,0},{6,2},{8,12},{10,14},{12,8},{14,10},{16,20},{18,... | collective-permute-start | bytes 3538952 | tf_op jit(solution)/shard_map/ppermute | solution.py:292
  345.0 15.5 %collective-permute-start.29 = (f32[2,2,48,384]{3,2,1,0:T(8,128)S(1)}, f32[2,2,48,384]{3,2,1,0:T(8,128)S(1)}, u32[]{:S(2)}, u32[]{:S(2)}) collective-permute-start(f32[2,2,48,384]{3,2,1,0:T(8,128)S(1)} %add_add_fusion.4), channel_id=1, source_target_pairs={{0,16},{2,18},{4,20},{6,22},{8,24},{10,26},{12,28},{14,30},{16,0},... | collective-permute-start | bytes 884744 | tf_op jit(solution)/shard_map/ppermute | solution.py:292
  360.5 67.8 %collective-permute-start.30 = (f32[2,2,96,384]{3,2,1,0:T(8,128)S(1)}, f32[2,2,96,384]{3,2,1,0:T(8,128)S(1)}, u32[]{:S(2)}, u32[]{:S(2)}) collective-permute-start(f32[2,2,96,384]{3,2,1,0:T(8,128)S(1)} %maximum_select_fusion.21), channel_id=1, source_target_pairs={{0,8},{2,10},{4,12},{6,14},{8,0},{10,2},{12,4},{14,6},{16,24},{18,... | collective-permute-start | bytes 1769480 | tf_op jit(solution)/shard_map/ppermute | solution.py:292
  394.6 27.3 %collective-permute-start.11 = (f32[2,384,384]{2,1,0:T(8,128)S(1)}, f32[2,384,384]{2,1,0:T(8,128)S(1)}, u32[]{:S(2)}, u32[]{:S(2)}) collective-permute-start(f32[2,384,384]{2,1,0:T(8,128)S(1)} %fusion.26), channel_id=1, source_target_pairs={{0,2},{2,0},{4,6},{6,4},{8,10},{10,8},{12,14},{14,12},{16,18},{18,... | collective-permute-start | bytes 3538952 | tf_op jit(solution)/shard_map/ppermute | solution.py:292
  397.3 27.1 %collective-permute-start.12 = (f32[2,384,384]{2,1,0:T(8,128)S(1)}, f32[2,384,384]{2,1,0:T(8,128)S(1)}, u32[]{:S(2)}, u32[]{:S(2)}) collective-permute-start(f32[2,384,384]{2,1,0:T(8,128)S(1)} %fusion.25), channel_id=1, source_target_pairs={{0,4},{2,6},{4,0},{6,2},{8,12},{10,14},{12,8},{14,10},{16,20},{18,... | collective-permute-start | bytes 3538952 | tf_op jit(solution)/shard_map/ppermute | solution.py:292
  421.9 90.0 %collective-permute-start.5 = (f32[1024,768]{0,1:T(8,128)}, f32[1024,768]{0,1:T(8,128)}, u32[]{:S(2)}, u32[]{:S(2)}) collective-permute-start(f32[1024,768]{0,1:T(8,128)} %add_add_fusion), channel_id=1, source_target_pairs={{0,1},{1,0},{2,3},{3,2},{4,5},{5,4},{6,7},{7,6},{8,9},{9,8},{10,11... | collective-permute-start | bytes 9437192 | tf_op jit(solution)/shard_map/ppermute | solution.py:298
  425.0 16.3 %collective-permute-start.14 = (f32[2,192,384]{2,1,0:T(8,128)S(1)}, f32[2,192,384]{2,1,0:T(8,128)S(1)}, u32[]{:S(2)}, u32[]{:S(2)}) collective-permute-start(f32[2,192,384]{2,1,0:T(8,128)S(1)} %get-tuple-element.113), channel_id=1, source_target_pairs={{0,2},{2,0},{4,6},{6,4},{8,10},{10,8},{12,14},{14,12},{16,18},{18,... | collective-permute-start | bytes 1769480 | tf_op jit(solution)/shard_map/ppermute | solution.py:292
  428.3 38.3 %collective-permute-start.56 = (f32[384,768]{1,0:T(8,128)S(1)}, f32[384,768]{1,0:T(8,128)S(1)}, u32[]{:S(2)}, u32[]{:S(2)}) collective-permute-start(f32[384,768]{1,0:T(8,128)S(1)} %maximum_select_fusion.18), channel_id=1, source_target_pairs={{0,2},{2,0},{4,6},{6,4},{8,10},{10,8},{12,14},{14,12},{16,18},{18,... | collective-permute-start | bytes 3538952 | tf_op jit(solution)/shard_map/ppermute | solution.py:292
  441.5 26.5 %collective-permute-start.15 = (f32[2,2,96,384]{3,2,1,0:T(8,128)S(1)}, f32[2,2,96,384]{3,2,1,0:T(8,128)S(1)}, u32[]{:S(2)}, u32[]{:S(2)}) collective-permute-start(f32[2,2,96,384]{3,2,1,0:T(8,128)S(1)} %get-tuple-element.133), channel_id=1, source_target_pairs={{0,8},{2,10},{4,12},{6,14},{8,0},{10,2},{12,4},{14,6},{16,24},{18,... | collective-permute-start | bytes 1769480 | tf_op jit(solution)/shard_map/ppermute | solution.py:292
  451.6 53.9 %collective-permute-start.32 = (f32[2,384,384]{2,1,0:T(8,128)}, f32[2,384,384]{2,1,0:T(8,128)}, u32[]{:S(2)}, u32[]{:S(2)}) collective-permute-start(f32[2,384,384]{2,1,0:T(8,128)} %maximum_select_fusion.12), channel_id=1, source_target_pairs={{0,2},{2,0},{4,6},{6,4},{8,10},{10,8},{12,14},{14,12},{16,18},{18,... | collective-permute-start | bytes 3538952 | tf_op jit(solution)/shard_map/ppermute | solution.py:292
  466.8 35.4 %collective-permute-start.33 = (f32[2,192,384]{2,1,0:T(8,128)S(1)}, f32[2,192,384]{2,1,0:T(8,128)}, u32[]{:S(2)}, u32[]{:S(2)}) collective-permute-start(f32[2,192,384]{2,1,0:T(8,128)S(1)} %get-tuple-element.138), channel_id=1, source_target_pairs={{0,2},{2,0},{4,6},{6,4},{8,10},{10,8},{12,14},{14,12},{16,18},{18,... | collective-permute-start | bytes 1769480 | tf_op jit(solution)/shard_map/ppermute | solution.py:292
  468.0 16.0 %collective-permute-start.16 = (f32[2,2,48,384]{3,2,1,0:T(8,128)S(1)}, f32[2,2,48,384]{3,2,1,0:T(8,128)}, u32[]{:S(2)}, u32[]{:S(2)}) collective-permute-start(f32[2,2,48,384]{3,2,1,0:T(8,128)S(1)} %dynamic-slice_add_fusion.7), channel_id=1, source_target_pairs={{0,16},{2,18},{4,20},{6,22},{8,24},{10,26},{12,28},{14,30},{16,0},... | collective-permute-start | bytes 884744 | tf_op jit(solution)/shard_map/ppermute | solution.py:292
  485.2 23.3 %collective-permute-start.17 = (f32[2,2,48,384]{3,2,1,0:T(8,128)S(1)}, f32[2,2,48,384]{3,2,1,0:T(8,128)S(1)}, u32[]{:S(2)}, u32[]{:S(2)}) collective-permute-start(f32[2,2,48,384]{3,2,1,0:T(8,128)S(1)} %add_add_fusion.5), channel_id=1, source_target_pairs={{0,16},{2,18},{4,20},{6,22},{8,24},{10,26},{12,28},{14,30},{16,0},... | collective-permute-start | bytes 884744 | tf_op jit(solution)/shard_map/ppermute | solution.py:292
  504.6 29.2 %collective-permute-start.34 = (f32[2,384,384]{2,1,0:T(8,128)}, f32[2,384,384]{2,1,0:T(8,128)}, u32[]{:S(2)}, u32[]{:S(2)}) collective-permute-start(f32[2,384,384]{2,1,0:T(8,128)} %maximum_select_fusion.13), channel_id=1, source_target_pairs={{0,4},{2,6},{4,0},{6,2},{8,12},{10,14},{12,8},{14,10},{16,20},{18,... | collective-permute-start | bytes 3538952 | tf_op jit(solution)/shard_map/ppermute | solution.py:292
  521.0 24.2 %collective-permute-start.19 = (f32[2,192,384]{2,1,0:T(8,128)S(1)}, f32[2,192,384]{2,1,0:T(8,128)}, u32[]{:S(2)}, u32[]{:S(2)}) collective-permute-start(f32[2,192,384]{2,1,0:T(8,128)S(1)} %get-tuple-element.141), channel_id=1, source_target_pairs={{0,4},{2,6},{4,0},{6,2},{8,12},{10,14},{12,8},{14,10},{16,20},{18,... | collective-permute-start | bytes 1769480 | tf_op jit(solution)/shard_map/ppermute | solution.py:292
  547.5 25.5 %collective-permute-start.20 = (f32[2,384,384]{2,1,0:T(8,128)}, f32[2,384,384]{2,1,0:T(8,128)}, u32[]{:S(2)}, u32[]{:S(2)}) collective-permute-start(f32[2,384,384]{2,1,0:T(8,128)} %maximum_select_fusion.9), channel_id=1, source_target_pairs={{0,2},{2,0},{4,6},{6,4},{8,10},{10,8},{12,14},{14,12},{16,18},{18,... | collective-permute-start | bytes 3538952 | tf_op jit(solution)/shard_map/ppermute | solution.py:292
  548.6 14.4 %collective-permute-start.10 = (f32[8,512]{1,0:T(8,128)S(1)}, f32[8,512]{1,0:T(8,128)S(1)}, u32[]{:S(2)}, u32[]{:S(2)}) collective-permute-start(f32[8,512]{1,0:T(8,128)S(1)} %add.401), channel_id=1, source_target_pairs={{0,16},{2,18},{4,20},{6,22},{8,24},{10,26},{12,28},{14,30},{16,0},... | collective-permute-start | bytes 49160 | tf_op jit(solution)/shard_map/ppermute | solution.py:292
  552.0 25.3 %collective-permute-start.22 = (f32[2,384,384]{2,1,0:T(8,128)}, f32[2,384,384]{2,1,0:T(8,128)}, u32[]{:S(2)}, u32[]{:S(2)}) collective-permute-start(f32[2,384,384]{2,1,0:T(8,128)} %maximum_select_fusion.10), channel_id=1, source_target_pairs={{0,4},{2,6},{4,0},{6,2},{8,12},{10,14},{12,8},{14,10},{16,20},{18,... | collective-permute-start | bytes 3538952 | tf_op jit(solution)/shard_map/ppermute | solution.py:292
  (74 other events, 534.4 us)
